TPU v7x, 256 devices: a whole 4x4x8 slice. The times are simulated.
256 devices in a mesh: dp: 8 (over z_hi, core), seq: 32 (over x, z_lo, y).
Axes of the slice: x: 4, y: 4, z: 8 (z_hi: 4, z_lo: 2; z = z_hi * 2 + z_lo), core: 2. Of those that a mesh axis runs over, the one named last changes fastest.
Arguments:
- normed: bfloat16 [8, 8192, 512], P('dp', 'seq'), may hold values from -6 to 6
- query_states: bfloat16 [8, 8192, 512], P('dp', 'seq'), may hold values from -6 to 6
- key_states: bfloat16 [8, 8192, 512], P('dp', 'seq'), may hold values from -6 to 6
- value_states: bfloat16 [8, 8192, 512], P('dp', 'seq'), may hold values from -6 to 6
- grad_output: bfloat16 [8, 8192, 512], P('dp', 'seq'), may hold values from -6 to 6
- w_qkv: bfloat16 [512, 1536], replicated, may hold values from -0.25 to 0.25
- w_out: bfloat16 [512, 512], replicated, may hold values from -0.25 to 0.25
- scene_tiles: int32 [8, 32], P('dp'), may hold values from 1 to 64, 256 in all within a row
Outputs:
- grad_normed: bfloat16 [8, 8192, 512], P('dp', 'seq')
- grad_w_qkv: float32 [512, 1536], replicated
- grad_w_out: float32 [512, 512], replicated
Inputs may be any that keep to these rules, and one draw needn't show every extreme that they name: `scene_tiles`: each row sums to 256; the largest entry of each row is exactly 64.
All inputs are finite; a program needn't handle non-finite values.
Results may differ from a plain program's by a relative error of at most 0.025.
Values may be sent and summed in bfloat16 or wider, within the bound.
No kernel may reach another device: no remote copies, remote signals or barrier semaphores. Data moves between devices by JAX's collectives and lax.ppermute only.
A program may use at most 128 MiB of HBM per device.

v0:
```python
import jax
import jax.numpy as jnp
from jax import lax
from jax.sharding import PartitionSpec as P

HEADS = 8
TILE = 32
REACH = 8


def shifted_2(x, axis, by):
    devices = lax.axis_size(axis)
    pairs = [(i, i + by) for i in range(devices) if 0 <= i + by < devices]
    return lax.ppermute(x, axis, pairs)


def batched(form, left, right):
    return jnp.einsum(form, left, right, preferred_element_type=jnp.float32)


def scene_of(scene_ends, positions):
    passed = (scene_ends[None, :] <= positions[:, None]).astype(jnp.int32)
    return jnp.sum(passed, axis=1)


def piece_mask(scene_ends, query_scene, device, device_count, tok_rows):
    inside = jnp.logical_and(device >= 0, device < device_count)
    key_scene = scene_of(scene_ends, device * tok_rows + jnp.arange(tok_rows, dtype=jnp.int32))
    allowed = jnp.logical_and(inside, query_scene[:, None] == key_scene[None, :])
    intersection = jnp.logical_and(key_scene[0] <= query_scene[-1], key_scene[-1] >= query_scene[0])
    return (allowed, jnp.logical_and(inside, intersection))


def block_grads(
    query3, grad_rows, w_out, window, first_device, device_count, scene_ends, query_scene
):
    tok_rows, head_count, head_size = query3.shape
    model_width = head_count * head_size
    score_scale = head_size ** (-0.5)
    piece_total = window.shape[0]

    def scores_of(piece):
        key3 = window[piece, 0].reshape(tok_rows, head_count, head_size)
        return batched("qhe,khe->hqk", query3, key3) * score_scale

    def geometry(piece):
        return piece_mask(scene_ends, query_scene, first_device + piece, device_count, tok_rows)

    def first_step(piece, carry_in):
        piece = jnp.asarray(piece).astype(jnp.int32)
        allowed, shared = geometry(piece)

        def first_update(carried):
            old_max, old_sum, accum = carried
            masked = jnp.where(allowed[None], scores_of(piece), -1e30)
            tile_max = jnp.max(masked, axis=2)
            exp_terms = jnp.where(allowed[None], jnp.exp(masked - tile_max[:, :, None]), 0.0)
            tile_sum = jnp.sum(exp_terms, axis=2)
            value3 = window[piece, 1].reshape(tok_rows, head_count, head_size)
            partial_value = batched("hqk,khe->qhe", exp_terms.astype(jnp.bfloat16), value3)
            new_max = jnp.maximum(old_max, tile_max)
            old_factor = jnp.exp(old_max - new_max)
            tile_factor = jnp.exp(tile_max - new_max)
            new_sum = old_sum * old_factor + tile_sum * tile_factor
            new_accum = accum * old_factor.T[:, :, None] + partial_value * tile_factor.T[:, :, None]
            return (new_max, new_sum, new_accum)

        return lax.cond(shared, first_update, lambda carried: carried, carry_in)

    start_max = jnp.full((head_count, tok_rows), -1e30, jnp.float32)
    start_sum = jnp.zeros((head_count, tok_rows), jnp.float32)
    start_accum = jnp.zeros((tok_rows, head_count, head_size), jnp.float32)
    run_max, run_sum, out_sum = lax.fori_loop(
        0, piece_total, first_step, (start_max, start_sum, start_accum)
    )

    def probs_of(piece, allowed):
        shifted = jnp.exp(scores_of(piece) - run_max[:, :, None]) / run_sum[:, :, None]
        return jnp.where(allowed[None], shifted, 0.0)

    attended = (out_sum / run_sum.T[:, :, None]).astype(jnp.bfloat16).reshape(tok_rows, model_width)
    grad_att = lax.dot_general(
        grad_rows, w_out, (((1,), (1,)), ((), ())), preferred_element_type=jnp.float32
    ).astype(jnp.bfloat16)
    grad3 = grad_att.reshape(tok_rows, head_count, head_size)
    att3 = attended.reshape(tok_rows, head_count, head_size)
    row_dots = jnp.sum(grad3.astype(jnp.float32) * att3.astype(jnp.float32), axis=2).T

    def grad_step(accum, piece):
        allowed, shared = geometry(piece)

        def grad_update(carried):
            softmax_rows = probs_of(piece, allowed)
            weights = softmax_rows.astype(jnp.bfloat16)
            key3 = window[piece, 0].reshape(tok_rows, head_count, head_size)
            value3 = window[piece, 1].reshape(tok_rows, head_count, head_size)
            grad_probs = batched("qhe,khe->hqk", grad3, value3)
            grad_scores = (softmax_rows * (grad_probs - row_dots[:, :, None]) * score_scale).astype(
                jnp.bfloat16
            )
            new_carried = carried + batched("hqk,khe->qhe", grad_scores, key3)
            grad_keys = (
                batched("hqk,qhe->khe", grad_scores, query3)
                .astype(jnp.bfloat16)
                .reshape(tok_rows, model_width)
            )
            grad_values = (
                batched("hqk,qhe->khe", weights, grad3)
                .astype(jnp.bfloat16)
                .reshape(tok_rows, model_width)
            )
            return (new_carried, jnp.stack([grad_keys, grad_values]))

        def passby(carried):
            return (carried, jnp.zeros((2, tok_rows, model_width), jnp.bfloat16))

        return lax.cond(shared, grad_update, passby, accum)

    grad_sum, grad_terms = lax.scan(
        grad_step,
        jnp.zeros((tok_rows, head_count, head_size), jnp.float32),
        jnp.arange(piece_total, dtype=jnp.int32),
    )
    return (grad_sum.astype(jnp.bfloat16).reshape(tok_rows, model_width), attended, grad_terms)


def local(normed, query_states, key_states, value_states, grad_output, w_qkv, w_out, scene_tiles):
    tok_rows = query_states.shape[1]
    model_width = query_states.shape[2]
    head_count = HEADS
    head_size = model_width // head_count
    seq_count = lax.axis_size("seq")
    my_index = lax.axis_index("seq")
    reach_span = REACH
    scene_ends = jnp.cumsum(scene_tiles[0]) * TILE
    query_scene = scene_of(scene_ends, my_index * tok_rows + jnp.arange(tok_rows, dtype=jnp.int32))
    kv_pair = jnp.concatenate([key_states, value_states], axis=0)
    pieces = {0: kv_pair}
    for offset in range(-reach_span, reach_span + 1):
        if offset != 0:
            pieces[offset] = shifted_2(kv_pair, "seq", -offset)
    window = jnp.stack([pieces[offset] for offset in range(-reach_span, reach_span + 1)])
    query3 = query_states[0].reshape(tok_rows, head_count, head_size)
    grad_query, attended, grad_terms = block_grads(
        query3,
        grad_output[0],
        w_out,
        window,
        my_index - reach_span,
        seq_count,
        scene_ends,
        query_scene,
    )
    summed = grad_terms[reach_span].astype(jnp.float32)
    for offset in range(-reach_span, reach_span + 1):
        if offset != 0:
            arrived = shifted_2(grad_terms[offset + reach_span], "seq", offset)
            summed = summed + arrived.astype(jnp.float32)
    grad_pairs = summed.astype(jnp.bfloat16)
    grad_qkv = jnp.concatenate([grad_query, grad_pairs[0], grad_pairs[1]], axis=1)
    w_grad_qkv = lax.dot_general(
        normed[0], grad_qkv, (((0,), (0,)), ((), ())), preferred_element_type=jnp.float32
    )
    w_grad_out = lax.dot_general(
        attended, grad_output[0], (((0,), (0,)), ((), ())), preferred_element_type=jnp.float32
    )
    grad_in = lax.dot_general(
        grad_qkv, w_qkv, (((1,), (1,)), ((), ())), preferred_element_type=jnp.float32
    ).astype(jnp.bfloat16)
    total_qkv, total_out = lax.psum((w_grad_qkv, w_grad_out), ("dp", "seq"))
    return (grad_in[None], total_qkv, total_out)


def solution(mesh):
    in_specs = (
        P("dp", "seq", None),
        P("dp", "seq", None),
        P("dp", "seq", None),
        P("dp", "seq", None),
        P("dp", "seq", None),
        P(),
        P(),
        P("dp", None),
    )
    out_specs = (P("dp", "seq", None), P(), P())
    return jax.shard_map(local, mesh=mesh, in_specs=in_specs, out_specs=out_specs, check_vma=False)
```

profile of v0, /device:TPU:1, one launch (start us, length us, event | category | flops | bytes accessed | tf_op | source)
XLA Modules:
  0.0 944.3 jit_solution(5051002058415824031)
XLA Ops:
  9.6 4.7 collective-permute-start
  14.4 6.8 collective-permute-start.1
  21.1 3.2 collective-permute-start.2
  27.1 3.6 collective-permute-start.4
  37.8 45.5 %collective-permute-start.6 = (bf16[2,256,512]{1,2,0:T(8,128)(2,1)S(1)}, bf16[2,256,512]{1,2,0:T(8,128)(2,1)S(1)}, u32[]{:S(2)}, u32[]{:S(2)}) collective-permute-start(bf16[2,256,512]{1,2,0:T(8,128)(2,1)S(1)} %pad_maximum_fusion.1), channel_id=1, source_target_pairs={{0,2},{1,3},{2,4},{3,5},{4,6},{5,7},{6,8},{7,9},{8,10},{9,11},{10,... | collective-permute-start | bytes 1572872 | tf_op jit(solution)/shard_map/ppermute | solution.py:14
  84.4 6.9 collective-permute-start.7
  100.0 3.2 collective-permute-done.7
  104.5 32.3 %collective-permute-done.8 = bf16[2,256,512]{1,2,0:T(8,128)(2,1)S(1)} collective-permute-done((bf16[2,256,512]{1,2,0:T(8,128)(2,1)S(1)}, bf16[2,256,512]{1,2,0:T(8,128)(2,1)S(1)}, u32[]{:S(2)}, u32[]{:S(2)}) %collective-permute-start.8) | collective-permute-done | bytes 524320 | tf_op jit(solution)/shard_map/ppermute | solution.py:14
  138.1 7.5 collective-permute-done.9
  148.3 5.3 collective-permute-done.11
  153.7 18.1 %collective-permute-done.12 = bf16[2,256,512]{1,2,0:T(8,128)(2,1)S(1)} collective-permute-done((bf16[2,256,512]{1,2,0:T(8,128)(2,1)S(1)}, bf16[2,256,512]{1,2,0:T(8,128)(2,1)S(1)}, u32[]{:S(2)}, u32[]{:S(2)}) %collective-permute-start.12) | collective-permute-done | bytes 524320 | tf_op jit(solution)/shard_map/ppermute | solution.py:14
  174.7 16.9 %collective-permute-done.15 = bf16[2,256,512]{1,2,0:T(8,128)(2,1)S(1)} collective-permute-done((bf16[2,256,512]{1,2,0:T(8,128)(2,1)S(1)}, bf16[2,256,512]{1,2,0:T(8,128)(2,1)S(1)}, u32[]{:S(2)}, u32[]{:S(2)}) %collective-permute-start.15) | collective-permute-done | bytes 524320 | tf_op jit(solution)/shard_map/ppermute | solution.py:14
  191.7 3.4 copy-done.1
  195.1 65.7 %while.32 = (s32[]{:T(128)}, f32[8,256]{1,0:T(8,128)S(1)}, f32[8,256]{1,0:T(8,128)S(1)}, f32[256,8,64]{0,2,1:T(8,128)S(1)}, s32[]{:T(128)}, /*index=5*/s32[32]{0...) while((s32[]{:T(128)}, f32[8,256]{1,0:T(8,128)S(1)}, ...), condition=%wide.region_8.9_spmd, body=%wide.region_2.8_spmd.sunk | while | flops 141592592 | bytes 9598482 | solution.py:73
  225.1 3.0 conditional.4
  261.0 109.3 %while.33 = (s32[]{:T(128)}, f32[256,8,64]{0,2,1:T(8,128)S(1)}, bf16[17,2,256,512]{2,3,1,0:T(8,128)(2,1)}, s32[17]{0:T(128)S(1)}, s32[]{:T(128)}, /*index=5*/s32...) while((s32[]{:T(128)}, f32[256,8,64]{0,2,1:T(8,128)S(1)}, ...), condition=%wide.region_14.15_spmd, body=%wide.region_10.14_spmd.sunk | while | flops 341073920 | bytes 16152614 | solution.py:119
  309.1 5.6 conditional.5
  320.1 5.6 conditional.5
  331.1 5.6 conditional.5
  370.3 3.8 slice_bitcast_fusion.15
  380.6 3.4 collective-permute-done.16
  385.3 7.0 collective-permute-done.17
  394.9 21.0 %collective-permute-done.19 = bf16[2,256,512]{1,2,0:T(8,128)(2,1)S(1)} collective-permute-done((bf16[2,256,512]{1,2,0:T(8,128)(2,1)S(1)}, bf16[2,256,512]{1,2,0:T(8,128)(2,1)S(1)}, u32[]{:S(2)}, u32[]{:S(2)}) %collective-permute-start.19) | collective-permute-done | bytes 524320 | tf_op jit(solution)/shard_map/ppermute | solution.py:14
  417.2 7.0 collective-permute-done.20
  425.6 76.8 %collective-permute-start.26 = (bf16[2,256,512]{1,2,0:T(8,128)(2,1)S(1)}, bf16[2,256,512]{1,2,0:T(8,128)(2,1)S(1)}, u32[]{:S(2)}, u32[]{:S(2)}) collective-permute-start(bf16[2,256,512]{1,2,0:T(8,128)(2,1)S(1)} %get-tuple-element.419), channel_id=1, source_target_pairs={{0,3},{1,4},{2,5},{3,6},{4,7},{5,8},{6,9},{7,10},{8,11},{9,12},{10... | collective-permute-start | bytes 1572872 | tf_op jit(solution)/shard_map/ppermute | solution.py:14
  502.4 21.5 %collective-permute-start.27 = (bf16[2,256,512]{1,2,0:T(8,128)(2,1)S(1)}, bf16[2,256,512]{1,2,0:T(8,128)(2,1)S(1)}, u32[]{:S(2)}, u32[]{:S(2)}) collective-permute-start(bf16[2,256,512]{1,2,0:T(8,128)(2,1)S(1)} %get-tuple-element.418), channel_id=1, source_target_pairs={{0,4},{1,5},{2,6},{3,7},{4,8},{5,9},{6,10},{7,11},{8,12},{9,13},{1... | collective-permute-start | bytes 1572872 | tf_op jit(solution)/shard_map/ppermute | solution.py:14
  526.4 9.7 %collective-permute-start.29 = (bf16[2,256,512]{1,2,0:T(8,128)(2,1)S(1)}, bf16[2,256,512]{1,2,0:T(8,128)(2,1)S(1)}, u32[]{:S(2)}, u32[]{:S(2)}) collective-permute-start(bf16[2,256,512]{1,2,0:T(8,128)(2,1)S(1)} %get-tuple-element.416), channel_id=1, source_target_pairs={{0,6},{1,7},{2,8},{3,9},{4,10},{5,11},{6,12},{7,13},{8,14},{9,15},... | collective-permute-start | bytes 1572872 | tf_op jit(solution)/shard_map/ppermute | solution.py:14
  536.1 42.0 %collective-permute-start.30 = (bf16[2,256,512]{1,2,0:T(8,128)(2,1)S(1)}, bf16[2,256,512]{1,2,0:T(8,128)(2,1)S(1)}, u32[]{:S(2)}, u32[]{:S(2)}) collective-permute-start(bf16[2,256,512]{1,2,0:T(8,128)(2,1)S(1)} %get-tuple-element.415), channel_id=1, source_target_pairs={{0,7},{1,8},{2,9},{3,10},{4,11},{5,12},{6,13},{7,14},{8,15},{9,16}... | collective-permute-start | bytes 1572872 | tf_op jit(solution)/shard_map/ppermute | solution.py:14
  581.0 6.4 collective-permute-done.30
  587.4 21.3 %collective-permute-done.31 = bf16[2,256,512]{1,2,0:T(8,128)(2,1)S(1)} collective-permute-done((bf16[2,256,512]{1,2,0:T(8,128)(2,1)S(1)}, bf16[2,256,512]{1,2,0:T(8,128)(2,1)S(1)}, u32[]{:S(2)}, u32[]{:S(2)}) %collective-permute-start.31) | collective-permute-done | bytes 524320 | tf_op jit(solution)/shard_map/ppermute | solution.py:14
  614.6 318.3 %all-reduce.3.cloned.1.call-done = (f32[512,1536]{0,1:T(8,128)}, f32[512,512]{1,0:T(8,128)}) async-done(((f32[512,1536]{0,1:T(8,128)}, f32[512,512]{1,0:T(8,128)}), (f32[512,1536]{0,1:T(8,128)}, f32[512,512]{1,0:T(8,128)})) %all-reduce.3.cloned.1.call-update) | async-done | bytes 4194320 | tf_op jit(solution)/shard_map/psum | solution.py:170
  932.9 3.6 copy.44
  (327 shorter events, 133.0 us)
Async XLA Ops:
  7.2 925.7 %all-reduce.3.cloned.1.call-start = ((), (), s32[]{:S(2)}) async-start(), calls=%async_computation | async-start | bytes 8388608 | tf_op jit(solution)/shard_map/psum | solution.py:170
  9.6 23.2 %collective-permute-start = (bf16[2,256,512]{1,2,0:T(8,128)(2,1)S(1)}, bf16[2,256,512]{1,2,0:T(8,128)(2,1)}, u32[]{:S(2)}, u32[]{:S(2)}) collective-permute-start(bf16[2,256,512]{1,2,0:T(8,128)(2,1)S(1)} %pad_maximum_fusion.1), channel_id=1, source_target_pairs={{0,8},{1,9},{2,10},{3,11},{4,12},{5,13},{6,14},{7,15},{8,16},{9,17... | collective-permute-start | bytes 1572872 | tf_op jit(solution)/shard_map/ppermute | solution.py:14
  14.4 23.5 %collective-permute-start.1 = (bf16[2,256,512]{1,2,0:T(8,128)(2,1)S(1)}, bf16[2,256,512]{1,2,0:T(8,128)(2,1)}, u32[]{:S(2)}, u32[]{:S(2)}) collective-permute-start(bf16[2,256,512]{1,2,0:T(8,128)(2,1)S(1)} %pad_maximum_fusion.1), channel_id=1, source_target_pairs={{0,7},{1,8},{2,9},{3,10},{4,11},{5,12},{6,13},{7,14},{8,15},{9,16}... | collective-permute-start | bytes 1572872 | tf_op jit(solution)/shard_map/ppermute | solution.py:14
  21.1 63.3 %collective-permute-start.2 = (bf16[2,256,512]{1,2,0:T(8,128)(2,1)S(1)}, bf16[2,256,512]{1,2,0:T(8,128)(2,1)}, u32[]{:S(2)}, u32[]{:S(2)}) collective-permute-start(bf16[2,256,512]{1,2,0:T(8,128)(2,1)S(1)} %pad_maximum_fusion.1), channel_id=1, source_target_pairs={{0,6},{1,7},{2,8},{3,9},{4,10},{5,11},{6,12},{7,13},{8,14},{9,15},... | collective-permute-start | bytes 1572872 | tf_op jit(solution)/shard_map/ppermute | solution.py:14
  24.3 68.1 %collective-permute-start.3 = (bf16[2,256,512]{1,2,0:T(8,128)(2,1)S(1)}, bf16[2,256,512]{1,2,0:T(8,128)(2,1)}, u32[]{:S(2)}, u32[]{:S(2)}) collective-permute-start(bf16[2,256,512]{1,2,0:T(8,128)(2,1)S(1)} %pad_maximum_fusion.1), channel_id=1, source_target_pairs={{0,5},{1,6},{2,7},{3,8},{4,9},{5,10},{6,11},{7,12},{8,13},{9,14},{... | collective-permute-start | bytes 1572872 | tf_op jit(solution)/shard_map/ppermute | solution.py:14
  27.1 67.7 %collective-permute-start.4 = (bf16[2,256,512]{1,2,0:T(8,128)(2,1)S(1)}, bf16[2,256,512]{1,2,0:T(8,128)(2,1)}, u32[]{:S(2)}, u32[]{:S(2)}) collective-permute-start(bf16[2,256,512]{1,2,0:T(8,128)(2,1)S(1)} %pad_maximum_fusion.1), channel_id=1, source_target_pairs={{0,4},{1,5},{2,6},{3,7},{4,8},{5,9},{6,10},{7,11},{8,12},{9,13},{1... | collective-permute-start | bytes 1572872 | tf_op jit(solution)/shard_map/ppermute | solution.py:14
  32.8 64.4 %collective-permute-start.5 = (bf16[2,256,512]{1,2,0:T(8,128)(2,1)S(1)}, bf16[2,256,512]{1,2,0:T(8,128)(2,1)S(1)}, u32[]{:S(2)}, u32[]{:S(2)}) collective-permute-start(bf16[2,256,512]{1,2,0:T(8,128)(2,1)S(1)} %pad_maximum_fusion.1), channel_id=1, source_target_pairs={{0,3},{1,4},{2,5},{3,6},{4,7},{5,8},{6,9},{7,10},{8,11},{9,12},{10... | collective-permute-start | bytes 1572872 | tf_op jit(solution)/shard_map/ppermute | solution.py:14
  37.8 60.8 %collective-permute-start.6 = (bf16[2,256,512]{1,2,0:T(8,128)(2,1)S(1)}, bf16[2,256,512]{1,2,0:T(8,128)(2,1)S(1)}, u32[]{:S(2)}, u32[]{:S(2)}) collective-permute-start(bf16[2,256,512]{1,2,0:T(8,128)(2,1)S(1)} %pad_maximum_fusion.1), channel_id=1, source_target_pairs={{0,2},{1,3},{2,4},{3,5},{4,6},{5,7},{6,8},{7,9},{8,10},{9,11},{10,... | collective-permute-start | bytes 1572872 | tf_op jit(solution)/shard_map/ppermute | solution.py:14
  84.4 18.7 %collective-permute-start.7 = (bf16[2,256,512]{1,2,0:T(8,128)(2,1)S(1)}, bf16[2,256,512]{1,2,0:T(8,128)(2,1)S(1)}, u32[]{:S(2)}, u32[]{:S(2)}) collective-permute-start(bf16[2,256,512]{1,2,0:T(8,128)(2,1)S(1)} %pad_maximum_fusion.1), channel_id=1, source_target_pairs={{0,1},{1,2},{2,3},{3,4},{4,5},{5,6},{6,7},{7,8},{8,9},{9,10},{10,1... | collective-permute-start | bytes 1572872 | tf_op jit(solution)/shard_map/ppermute | solution.py:14
  92.5 44.3 %collective-permute-start.8 = (bf16[2,256,512]{1,2,0:T(8,128)(2,1)S(1)}, bf16[2,256,512]{1,2,0:T(8,128)(2,1)S(1)}, u32[]{:S(2)}, u32[]{:S(2)}) collective-permute-start(bf16[2,256,512]{1,2,0:T(8,128)(2,1)S(1)} %pad_maximum_fusion.1), channel_id=1, source_target_pairs={{1,0},{2,1},{3,2},{4,3},{5,4},{6,5},{7,6},{8,7},{9,8},{10,9},{11,1... | collective-permute-start | bytes 1572872 | tf_op jit(solution)/shard_map/ppermute | solution.py:14
  94.9 50.7 %collective-permute-start.9 = (bf16[2,256,512]{1,2,0:T(8,128)(2,1)S(1)}, bf16[2,256,512]{1,2,0:T(8,128)(2,1)S(1)}, u32[]{:S(2)}, u32[]{:S(2)}) collective-permute-start(bf16[2,256,512]{1,2,0:T(8,128)(2,1)S(1)} %pad_maximum_fusion.1), channel_id=1, source_target_pairs={{2,0},{3,1},{4,2},{5,3},{6,4},{7,5},{8,6},{9,7},{10,8},{11,9},{12,... | collective-permute-start | bytes 1572872 | tf_op jit(solution)/shard_map/ppermute | solution.py:14
  97.3 49.7 %collective-permute-start.10 = (bf16[2,256,512]{1,2,0:T(8,128)(2,1)S(1)}, bf16[2,256,512]{1,2,0:T(8,128)(2,1)S(1)}, u32[]{:S(2)}, u32[]{:S(2)}) collective-permute-start(bf16[2,256,512]{1,2,0:T(8,128)(2,1)S(1)} %pad_maximum_fusion.1), channel_id=1, source_target_pairs={{3,0},{4,1},{5,2},{6,3},{7,4},{8,5},{9,6},{10,7},{11,8},{12,9},{13... | collective-permute-start | bytes 1572872 | tf_op jit(solution)/shard_map/ppermute | solution.py:14
  98.6 55.0 %collective-permute-start.11 = (bf16[2,256,512]{1,2,0:T(8,128)(2,1)S(1)}, bf16[2,256,512]{1,2,0:T(8,128)(2,1)S(1)}, u32[]{:S(2)}, u32[]{:S(2)}) collective-permute-start(bf16[2,256,512]{1,2,0:T(8,128)(2,1)S(1)} %pad_maximum_fusion.1), channel_id=1, source_target_pairs={{4,0},{5,1},{6,2},{7,3},{8,4},{9,5},{10,6},{11,7},{12,8},{13,9},{1... | collective-permute-start | bytes 1572872 | tf_op jit(solution)/shard_map/ppermute | solution.py:14
  103.1 68.6 %collective-permute-start.12 = (bf16[2,256,512]{1,2,0:T(8,128)(2,1)S(1)}, bf16[2,256,512]{1,2,0:T(8,128)(2,1)S(1)}, u32[]{:S(2)}, u32[]{:S(2)}) collective-permute-start(bf16[2,256,512]{1,2,0:T(8,128)(2,1)S(1)} %pad_maximum_fusion.1), channel_id=1, source_target_pairs={{5,0},{6,1},{7,2},{8,3},{9,4},{10,5},{11,6},{12,7},{13,8},{14,9},{... | collective-permute-start | bytes 1572872 | tf_op jit(solution)/shard_map/ppermute | solution.py:14
  136.8 37.9 %collective-permute-start.13 = (bf16[2,256,512]{1,2,0:T(8,128)(2,1)S(1)}, bf16[2,256,512]{1,2,0:T(8,128)(2,1)S(1)}, u32[]{:S(2)}, u32[]{:S(2)}) collective-permute-start(bf16[2,256,512]{1,2,0:T(8,128)(2,1)S(1)} %pad_maximum_fusion.1), channel_id=1, source_target_pairs={{6,0},{7,1},{8,2},{9,3},{10,4},{11,5},{12,6},{13,7},{14,8},{15,9},... | collective-permute-start | bytes 1572872 | tf_op jit(solution)/shard_map/ppermute | solution.py:14
  145.6 29.1 %collective-permute-start.14 = (bf16[2,256,512]{1,2,0:T(8,128)(2,1)S(1)}, bf16[2,256,512]{1,2,0:T(8,128)(2,1)S(1)}, u32[]{:S(2)}, u32[]{:S(2)}) collective-permute-start(bf16[2,256,512]{1,2,0:T(8,128)(2,1)S(1)} %pad_maximum_fusion.1), channel_id=1, source_target_pairs={{7,0},{8,1},{9,2},{10,3},{11,4},{12,5},{13,6},{14,7},{15,8},{16,9}... | collective-permute-start | bytes 1572872 | tf_op jit(solution)/shard_map/ppermute | solution.py:14
  146.9 44.7 %collective-permute-start.15 = (bf16[2,256,512]{1,2,0:T(8,128)(2,1)S(1)}, bf16[2,256,512]{1,2,0:T(8,128)(2,1)S(1)}, u32[]{:S(2)}, u32[]{:S(2)}) collective-permute-start(bf16[2,256,512]{1,2,0:T(8,128)(2,1)S(1)} %pad_maximum_fusion.1), channel_id=1, source_target_pairs={{8,0},{9,1},{10,2},{11,3},{12,4},{13,5},{14,6},{15,7},{16,8},{17,9... | collective-permute-start | bytes 1572872 | tf_op jit(solution)/shard_map/ppermute | solution.py:14
  375.4 16.9 %collective-permute-start.17 = (bf16[2,256,512]{1,2,0:T(8,128)(2,1)S(1)}, bf16[2,256,512]{1,2,0:T(8,128)(2,1)S(1)}, u32[]{:S(2)}, u32[]{:S(2)}) collective-permute-start(bf16[2,256,512]{1,2,0:T(8,128)(2,1)S(1)} %get-tuple-element.428), channel_id=1, source_target_pairs={{7,0},{8,1},{9,2},{10,3},{11,4},{12,5},{13,6},{14,7},{15,8},{16,9}... | collective-permute-start | bytes 1572872 | tf_op jit(solution)/shard_map/ppermute | solution.py:14
  376.7 16.9 %collective-permute-start.18 = (bf16[2,256,512]{1,2,0:T(8,128)(2,1)S(1)}, bf16[2,256,512]{1,2,0:T(8,128)(2,1)S(1)}, u32[]{:S(2)}, u32[]{:S(2)}) collective-permute-start(bf16[2,256,512]{1,2,0:T(8,128)(2,1)S(1)} %get-tuple-element.427), channel_id=1, source_target_pairs={{6,0},{7,1},{8,2},{9,3},{10,4},{11,5},{12,6},{13,7},{14,8},{15,9},... | collective-permute-start | bytes 1572872 | tf_op jit(solution)/shard_map/ppermute | solution.py:14
  378.0 37.9 %collective-permute-start.19 = (bf16[2,256,512]{1,2,0:T(8,128)(2,1)S(1)}, bf16[2,256,512]{1,2,0:T(8,128)(2,1)S(1)}, u32[]{:S(2)}, u32[]{:S(2)}) collective-permute-start(bf16[2,256,512]{1,2,0:T(8,128)(2,1)S(1)} %get-tuple-element.426), channel_id=1, source_target_pairs={{5,0},{6,1},{7,2},{8,3},{9,4},{10,5},{11,6},{12,7},{13,8},{14,9},{... | collective-permute-start | bytes 1572872 | tf_op jit(solution)/shard_map/ppermute | solution.py:14
  379.3 45.0 %collective-permute-start.20 = (bf16[2,256,512]{1,2,0:T(8,128)(2,1)S(1)}, bf16[2,256,512]{1,2,0:T(8,128)(2,1)S(1)}, u32[]{:S(2)}, u32[]{:S(2)}) collective-permute-start(bf16[2,256,512]{1,2,0:T(8,128)(2,1)S(1)} %get-tuple-element.425), channel_id=1, source_target_pairs={{4,0},{5,1},{6,2},{7,3},{8,4},{9,5},{10,6},{11,7},{12,8},{13,9},{1... | collective-permute-start | bytes 1572872 | tf_op jit(solution)/shard_map/ppermute | solution.py:14
  384.0 41.6 %collective-permute-start.21 = (bf16[2,256,512]{1,2,0:T(8,128)(2,1)S(1)}, bf16[2,256,512]{1,2,0:T(8,128)(2,1)S(1)}, u32[]{:S(2)}, u32[]{:S(2)}) collective-permute-start(bf16[2,256,512]{1,2,0:T(8,128)(2,1)S(1)} %get-tuple-element.424), channel_id=1, source_target_pairs={{3,0},{4,1},{5,2},{6,3},{7,4},{8,5},{9,6},{10,7},{11,8},{12,9},{13... | collective-permute-start | bytes 1572872 | tf_op jit(solution)/shard_map/ppermute | solution.py:14
  392.3 110.1 %collective-permute-start.22 = (bf16[2,256,512]{1,2,0:T(8,128)(2,1)S(1)}, bf16[2,256,512]{1,2,0:T(8,128)(2,1)S(1)}, u32[]{:S(2)}, u32[]{:S(2)}) collective-permute-start(bf16[2,256,512]{1,2,0:T(8,128)(2,1)S(1)} %get-tuple-element.423), channel_id=1, source_target_pairs={{2,0},{3,1},{4,2},{5,3},{6,4},{7,5},{8,6},{9,7},{10,8},{11,9},{12,... | collective-permute-start | bytes 1572872 | tf_op jit(solution)/shard_map/ppermute | solution.py:14
  393.6 130.3 %collective-permute-start.23 = (bf16[2,256,512]{1,2,0:T(8,128)(2,1)S(1)}, bf16[2,256,512]{1,2,0:T(8,128)(2,1)S(1)}, u32[]{:S(2)}, u32[]{:S(2)}) collective-permute-start(bf16[2,256,512]{1,2,0:T(8,128)(2,1)S(1)} %get-tuple-element.422), channel_id=1, source_target_pairs={{1,0},{2,1},{3,2},{4,3},{5,4},{6,5},{7,6},{8,7},{9,8},{10,9},{11,1... | collective-permute-start | bytes 1572872 | tf_op jit(solution)/shard_map/ppermute | solution.py:14
  415.9 110.5 %collective-permute-start.24 = (bf16[2,256,512]{1,2,0:T(8,128)(2,1)S(1)}, bf16[2,256,512]{1,2,0:T(8,128)(2,1)S(1)}, u32[]{:S(2)}, u32[]{:S(2)}) collective-permute-start(bf16[2,256,512]{1,2,0:T(8,128)(2,1)S(1)} %get-tuple-element.421), channel_id=1, source_target_pairs={{0,1},{1,2},{2,3},{3,4},{4,5},{5,6},{6,7},{7,8},{8,9},{9,10},{10,1... | collective-permute-start | bytes 1572872 | tf_op jit(solution)/shard_map/ppermute | solution.py:14
  424.3 111.8 %collective-permute-start.25 = (bf16[2,256,512]{1,2,0:T(8,128)(2,1)S(1)}, bf16[2,256,512]{1,2,0:T(8,128)(2,1)S(1)}, u32[]{:S(2)}, u32[]{:S(2)}) collective-permute-start(bf16[2,256,512]{1,2,0:T(8,128)(2,1)S(1)} %get-tuple-element.420), channel_id=1, source_target_pairs={{0,2},{1,3},{2,4},{3,5},{4,6},{5,7},{6,8},{7,9},{8,10},{9,11},{10,... | collective-permute-start | bytes 1572872 | tf_op jit(solution)/shard_map/ppermute | solution.py:14
  425.6 152.5 %collective-permute-start.26 = (bf16[2,256,512]{1,2,0:T(8,128)(2,1)S(1)}, bf16[2,256,512]{1,2,0:T(8,128)(2,1)S(1)}, u32[]{:S(2)}, u32[]{:S(2)}) collective-permute-start(bf16[2,256,512]{1,2,0:T(8,128)(2,1)S(1)} %get-tuple-element.419), channel_id=1, source_target_pairs={{0,3},{1,4},{2,5},{3,6},{4,7},{5,8},{6,9},{7,10},{8,11},{9,12},{10... | collective-permute-start | bytes 1572872 | tf_op jit(solution)/shard_map/ppermute | solution.py:14
  502.4 78.6 %collective-permute-start.27 = (bf16[2,256,512]{1,2,0:T(8,128)(2,1)S(1)}, bf16[2,256,512]{1,2,0:T(8,128)(2,1)S(1)}, u32[]{:S(2)}, u32[]{:S(2)}) collective-permute-start(bf16[2,256,512]{1,2,0:T(8,128)(2,1)S(1)} %get-tuple-element.418), channel_id=1, source_target_pairs={{0,4},{1,5},{2,6},{3,7},{4,8},{5,9},{6,10},{7,11},{8,12},{9,13},{1... | collective-permute-start | bytes 1572872 | tf_op jit(solution)/shard_map/ppermute | solution.py:14
  523.9 57.1 %collective-permute-start.28 = (bf16[2,256,512]{1,2,0:T(8,128)(2,1)S(1)}, bf16[2,256,512]{1,2,0:T(8,128)(2,1)S(1)}, u32[]{:S(2)}, u32[]{:S(2)}) collective-permute-start(bf16[2,256,512]{1,2,0:T(8,128)(2,1)S(1)} %get-tuple-element.417), channel_id=1, source_target_pairs={{0,5},{1,6},{2,7},{3,8},{4,9},{5,10},{6,11},{7,12},{8,13},{9,14},{... | collective-permute-start | bytes 1572872 | tf_op jit(solution)/shard_map/ppermute | solution.py:14
  526.4 54.5 %collective-permute-start.29 = (bf16[2,256,512]{1,2,0:T(8,128)(2,1)S(1)}, bf16[2,256,512]{1,2,0:T(8,128)(2,1)S(1)}, u32[]{:S(2)}, u32[]{:S(2)}) collective-permute-start(bf16[2,256,512]{1,2,0:T(8,128)(2,1)S(1)} %get-tuple-element.416), channel_id=1, source_target_pairs={{0,6},{1,7},{2,8},{3,9},{4,10},{5,11},{6,12},{7,13},{8,14},{9,15},... | collective-permute-start | bytes 1572872 | tf_op jit(solution)/shard_map/ppermute | solution.py:14
  536.1 51.3 %collective-permute-start.30 = (bf16[2,256,512]{1,2,0:T(8,128)(2,1)S(1)}, bf16[2,256,512]{1,2,0:T(8,128)(2,1)S(1)}, u32[]{:S(2)}, u32[]{:S(2)}) collective-permute-start(bf16[2,256,512]{1,2,0:T(8,128)(2,1)S(1)} %get-tuple-element.415), channel_id=1, source_target_pairs={{0,7},{1,8},{2,9},{3,10},{4,11},{5,12},{6,13},{7,14},{8,15},{9,16}... | collective-permute-start | bytes 1572872 | tf_op jit(solution)/shard_map/ppermute | solution.py:14
  578.1 30.6 %collective-permute-start.31 = (bf16[2,256,512]{1,2,0:T(8,128)(2,1)S(1)}, bf16[2,256,512]{1,2,0:T(8,128)(2,1)S(1)}, u32[]{:S(2)}, u32[]{:S(2)}) collective-permute-start(bf16[2,256,512]{1,2,0:T(8,128)(2,1)S(1)} %get-tuple-element.414), channel_id=1, source_target_pairs={{0,8},{1,9},{2,10},{3,11},{4,12},{5,13},{6,14},{7,15},{8,16},{9,17... | collective-permute-start | bytes 1572872 | tf_op jit(solution)/shard_map/ppermute | solution.py:14
  (8 other events, 912.9 us)
Sparse Core Ops, SparseCore 0:
  613.4 319.4 all-reduce.2
where the time goes:
time: 952 us; the launch traced here: 944 us
  waiting for transfers between devices  472 us (50%)
  starting transfers between devices  253 us (27%)
  loops' own time  105 us (11%)
  local copies, waits for them, and re-layouts  74.3 us (8%)
  matrix products  17.1 us (2%)
  between operations  14.7 us (2%)
    psum x1, waiting for transfers between devices, local(): total_qkv, total_out = lax.psum((w_grad_qkv, w_grad_out), ('dp', 'seq'))  318 us
    ppermute x32, starting transfers between devices, shifted_2(): return lax.ppermute(x, axis, pairs)  253 us
    ppermute x32, waiting for transfers between devices, shifted_2(): return lax.ppermute(x, axis, pairs)  154 us
    another operation x1, loops' own time, block_grads(): lax.scan(grad_step, jnp.zeros((tok_rows, head_count, head_size), jnp.floa...  54.3 us
    another operation x1, loops' own time, block_grads(): lax.fori_loop(0, piece_total, first_step, (start_max, start_sum, start_ac...  43.5 us
    slice x34, local copies, waits for them, and re-layouts, piece_mask(): query_scene[0]  22.8 us
  transfers between devices with their start and end apart: 33, of which 15 were waited for; matrix products, arithmetic and copies ran while one was open for 1% of the time, Pallas kernels for 0%

commit v1 on v0

v1 whole, which is shorter than its diff:
```python
import jax
import jax.numpy as jnp
from jax import lax
from jax.experimental import pallas as pl
from jax.experimental.pallas import tpu as pltpu
from jax.sharding import Mesh
from jax.sharding import PartitionSpec as P

HEADS = 8
HEAD = 64
TILE = 32
TOK = 256
SCENES = 32
BARRED = 16384.0
F32 = jnp.float32
BF16 = jnp.bfloat16
NT = (((1,), (1,)), ((), ()))
TN = (((0,), (0,)), ((), ()))
VMEM_LIMIT = 48 * 1024 * 1024


def params():
    return pltpu.CompilerParams(vmem_limit_bytes=VMEM_LIMIT)


def vmem():
    return pl.BlockSpec(memory_space=pltpu.VMEM)


def smem():
    return pl.BlockSpec(memory_space=pltpu.SMEM)


def dot(a, b, dims=(((1,), (0,)), ((), ()))):
    return lax.dot_general(a, b, dims, preferred_element_type=F32)


def pack_two(left, right, out_ref):
    for h in range(HEADS):
        cut = slice(h * HEAD, (h + 1) * HEAD)
        out_ref[h] = jnp.concatenate([left[:, cut], right[:, cut]], axis=1)


def pack_kv_kernel(k_ref, v_ref, out_ref):
    pack_two(k_ref[0], v_ref[0], out_ref)


def pack_qd_kernel(q_ref, g_ref, w_ref, out_ref):
    grad_att = dot(g_ref[0], w_ref[...], NT).astype(BF16)
    pack_two(q_ref[0], grad_att, out_ref)


def attention_kernel(
    tiles_ref, place_ref, own_ref, prev_ref, next_ref, qd_ref,
    aq_ref, kv_own_ref, kv_prev_ref, kv_next_ref,
    packed, keys, turned, scores, weights, totals,
):
    quarter = own_ref.shape[0]
    per_quarter = quarter // TOK
    blocks = 3 * per_quarter
    first_query = place_ref[0] * quarter
    first_key = first_query - quarter

    lane = lax.broadcasted_iota(jnp.int32, (1, 128), 1)
    low = lane < HEAD

    def read_scenes(s, carry):
        start, starts, ends, lows, highs = carry
        end = start + tiles_ref[0, s] * TILE
        mine = lane == HEAD + s
        starts = jnp.where(mine, start, starts)
        ends = jnp.where(mine, end, ends)
        new_lows, new_highs = [], []
        for i in range(per_quarter):
            head = first_query + i * TOK
            tail = head + TOK - 1
            new_lows.append(jnp.where(jnp.logical_and(start <= head, head < end), start, lows[i]))
            new_highs.append(jnp.where(jnp.logical_and(start <= tail, tail < end), end, highs[i]))
        return end, starts, ends, tuple(new_lows), tuple(new_highs)

    zero = jnp.int32(0)
    nowhere = jnp.full((1, 128), 2**30, jnp.int32)
    _, starts, ends, lows, highs = lax.fori_loop(
        0, SCENES, read_scenes, (zero, nowhere, nowhere, (zero,) * per_quarter, (zero,) * per_quarter)
    )
    firsts = [(x - first_key) // TOK for x in lows]
    lasts = [(x - first_key + TOK - 1) // TOK for x in highs]

    scene_lane = jnp.logical_and(lane >= HEAD, lane < HEAD + SCENES)
    rows = lax.broadcasted_iota(jnp.int32, (TOK, 1), 0)

    def prepare(source_ref, base):
        def body(j, _):
            block = source_ref[pl.ds(pl.multiple_of((j - base) * TOK, TOK), TOK), :]
            position = first_key + j * TOK + rows
            inside = jnp.logical_and(position >= starts, position < ends)
            mark = jnp.where(inside, 1.0, 0.0).astype(BF16)
            packed[j] = block
            keys[j] = jnp.where(low, block, mark)
            turned[j] = block.T
            return 0
        return body

    begin, finish = firsts[0], lasts[-1]
    for part, source in enumerate((prev_ref, own_ref, next_ref)):
        base = part * per_quarter
        lax.fori_loop(
            jnp.maximum(begin, base), jnp.minimum(finish, base + per_quarter), prepare(source, base), 0
        )
    totals[...] = jnp.zeros_like(totals)

    for i in range(per_quarter):
        span = slice(i * TOK, (i + 1) * TOK)
        qd = qd_ref[span, :]
        position = first_query + i * TOK + rows
        same = jnp.logical_and(position >= starts, position < ends)
        other = jnp.where(jnp.logical_and(scene_lane, jnp.logical_not(same)), -BARRED, 0.0)
        query = jnp.where(low, qd.astype(F32) * HEAD**-0.5, other).astype(BF16)
        nil = jnp.zeros_like(qd)
        only_q = jnp.where(low, (qd.astype(F32) * HEAD**-0.5).astype(BF16), nil)
        only_d = jnp.where(low, nil, qd)
        pair = jnp.concatenate([only_q, only_d], axis=0)

        def first_pass(j, top):
            s = dot(keys[j], query, NT)
            scores[j] = s
            return jnp.maximum(top, jnp.max(s.reshape(TOK // 8, 8, TOK), axis=0))

        top = lax.fori_loop(firsts[i], lasts[i], first_pass, jnp.full((8, TOK), -1e30, F32))
        top = jnp.max(top, axis=0, keepdims=True)

        def second_pass(j, carry):
            total, attended = carry
            p = jnp.exp(scores[j] - top)
            total = total + jnp.sum(p.reshape(TOK // 8, 8, TOK), axis=0)
            p = p.astype(BF16)
            weights[j] = p
            attended = attended + dot(turned[j, HEAD:, :], p)
            return total, attended

        total, attended = lax.fori_loop(
            firsts[i], lasts[i], second_pass, (jnp.zeros((8, TOK), F32), jnp.zeros((HEAD, TOK), F32))
        )
        share = 1.0 / jnp.sum(total, axis=0, keepdims=True)
        attended = (attended * share).astype(BF16).astype(F32)
        grad_turned = qd.T[HEAD:, :].astype(F32)
        row_dot = jnp.sum(attended * grad_turned, axis=0, keepdims=True)

        def third_pass(j, grad_query):
            grad_probs = dot(packed[j], only_d, NT)
            probs = weights[j].astype(F32) * share
            grad_scores = (probs * (grad_probs - row_dot)).astype(BF16)
            both = jnp.concatenate([grad_scores, probs.astype(BF16)], axis=1)
            totals[j] += dot(both, pair)
            return grad_query + dot(turned[j, :HEAD, :], grad_scores)

        grad_query = lax.fori_loop(firsts[i], lasts[i], third_pass, jnp.zeros((HEAD, TOK), F32))
        out = jnp.concatenate([attended, grad_query * HEAD**-0.5], axis=0)
        aq_ref[span, :] = out.T.astype(BF16)

    for part, out_ref in enumerate((kv_prev_ref, kv_own_ref, kv_next_ref)):
        for j in range(per_quarter):
            out_ref[j] = totals[part * per_quarter + j].astype(BF16)


def attention(scene_tiles, place, own, prev, after, qd):
    quarter = own.shape[0]
    blocks = 3 * quarter // TOK
    grads = jax.ShapeDtypeStruct((quarter // TOK, TOK, 2 * HEAD), BF16)
    return pl.pallas_call(
        attention_kernel,
        out_shape=(jax.ShapeDtypeStruct(own.shape, BF16), grads, grads, grads),
        in_specs=[smem(), smem()] + [vmem()] * 4,
        out_specs=(vmem(),) * 4,
        scratch_shapes=[
            pltpu.VMEM((blocks, TOK, 2 * HEAD), BF16),
            pltpu.VMEM((blocks, TOK, 2 * HEAD), BF16),
            pltpu.VMEM((blocks, 2 * HEAD, TOK), BF16),
            pltpu.VMEM((blocks, TOK, TOK), F32),
            pltpu.VMEM((blocks, TOK, TOK), BF16),
            pltpu.VMEM((blocks, TOK, 2 * HEAD), F32),
        ],
        compiler_params=params(),
        name="attention",
    )(scene_tiles, place, own, prev, after, qd)


def finish_kernel(
    core_ref, aq_ref, kv_ref, normed_ref, gout_ref, wqkv_ref, gin_ref, keep_ref, send_ref, att, joint
):
    width = HEADS * HEAD
    for h in range(0, HEADS, 2):
        pair = slice(h * HEAD, (h + 2) * HEAD)
        one, two = aq_ref[h], aq_ref[h + 1]
        att[:, pair] = jnp.concatenate([one[:, :HEAD], two[:, :HEAD]], axis=1)
        joint[:, pair] = jnp.concatenate([one[:, HEAD:], two[:, HEAD:]], axis=1)
        one, two = kv_ref[h], kv_ref[h + 1]
        pair = slice(width + h * HEAD, width + (h + 2) * HEAD)
        joint[:, pair] = jnp.concatenate([one[:, :HEAD], two[:, :HEAD]], axis=1)
        pair = slice(2 * width + h * HEAD, 2 * width + (h + 2) * HEAD)
        joint[:, pair] = jnp.concatenate([one[:, HEAD:], two[:, HEAD:]], axis=1)
    core = core_ref[0]
    grads = joint[...]
    gin_ref[0] = dot(grads, wqkv_ref[...], NT).astype(BF16)
    half = width // 2
    for out_ref, which in ((keep_ref, core), (send_ref, 1 - core)):
        cut = pl.ds(pl.multiple_of(which * half, half), half)
        out_ref[:, : 3 * width] = dot(normed_ref[0, :, cut], grads, TN).astype(BF16)
        out_ref[:, 3 * width :] = dot(att[:, cut], gout_ref[0], TN).astype(BF16)


def finish(core, aq, kv, normed, gout, wqkv):
    width = HEADS * HEAD
    part = jax.ShapeDtypeStruct((width // 2, 4 * width), BF16)
    return pl.pallas_call(
        finish_kernel,
        out_shape=(jax.ShapeDtypeStruct(normed.shape, BF16), part, part),
        in_specs=[smem()] + [vmem()] * 5,
        out_specs=(vmem(),) * 3,
        scratch_shapes=[pltpu.VMEM((TOK, width), BF16), pltpu.VMEM((TOK, 3 * width), BF16)],
        compiler_params=params(),
        name="finish",
    )(core, aq, kv, normed, gout, wqkv)


def pack(kernel, *arrays):
    return pl.pallas_call(
        kernel,
        out_shape=jax.ShapeDtypeStruct((HEADS, TOK, 2 * HEAD), BF16),
        in_specs=[vmem()] * len(arrays),
        out_specs=vmem(),
        compiler_params=params(),
        name="pack",
    )(*arrays)


def spread(x, axes, count):
    return lax.all_to_all(jnp.broadcast_to(x[None], (count,) + x.shape), axes, 0, 0, tiled=True)


def shift(x, by):
    count = lax.axis_size("x")
    return lax.ppermute(x, "x", [(i, i + by) for i in range(count) if 0 <= i + by < count])


def local(normed, query_states, key_states, value_states, grad_output, w_qkv, w_out, scene_tiles):
    heads_axes, seq_axes = ("zl", "y"), ("x", "zl", "y")
    seq_count = lax.axis_size(seq_axes)
    quarter_shape = (lax.axis_size(heads_axes) * TOK, 2 * HEAD)
    place = lax.axis_index("x").reshape(1).astype(jnp.int32)
    core = lax.axis_index("c").reshape(1).astype(jnp.int32)

    def exchange(x):
        return lax.all_to_all(x, heads_axes, 0, 0, tiled=True)

    own = exchange(pack(pack_kv_kernel, key_states, value_states)).reshape(quarter_shape)
    prev, after = shift(own, 1), shift(own, -1)
    qd = exchange(pack(pack_qd_kernel, query_states, grad_output, w_out)).reshape(quarter_shape)
    aq, kv_own, kv_prev, kv_next = attention(scene_tiles, place, own, prev, after, qd)
    from_next, from_prev = shift(kv_prev, -1), shift(kv_next, 1)
    aq = exchange(aq.reshape(HEADS, TOK, 2 * HEAD))
    kv = (kv_own.astype(F32) + from_next.astype(F32) + from_prev.astype(F32)).astype(BF16)
    kv = exchange(kv)
    grad_in, keep, send = finish(core, aq, kv, normed, grad_output, w_qkv)

    swap = [(0, 1), (1, 0)]
    came = lax.ppermute(send, "c", swap)
    part = (keep.astype(F32) + came.astype(F32)).astype(BF16)
    rows, columns = part.shape
    part = part.reshape(seq_count, rows // seq_count, columns)
    part = jnp.sum(lax.all_to_all(part, seq_axes, 0, 0, tiled=True).astype(F32), axis=0)
    part = jnp.sum(spread(part.astype(BF16), ("zh",), lax.axis_size("zh")).astype(F32)
                   .reshape((-1,) + part.shape), axis=0)
    mine = spread(part.astype(BF16), seq_axes, seq_count).reshape(rows, columns)
    other = lax.ppermute(mine, "c", swap)
    first = core[0] == 0
    total = jnp.concatenate([jnp.where(first, mine, other), jnp.where(first, other, mine)], axis=0)
    total = total.astype(F32)
    joint_width = w_qkv.shape[1]
    return grad_in, total[:, :joint_width], total[:, joint_width:]


def solution(mesh):
    fine = Mesh(mesh.devices.reshape(4, 2, 4, 2, 4), ("zh", "c", "x", "zl", "y"))
    dp, seq = ("zh", "c"), ("x", "zl", "y")
    rows = P(dp, seq, None)
    in_specs = (rows,) * 5 + (P(), P(), P(dp, None))
    return jax.shard_map(local, mesh=fine, in_specs=in_specs, out_specs=(rows, P(), P()), check_vma=False)
```

time: 952 us -> 209 us (0.22)
  waiting for transfers between devices: 472 us -> 35.7 us
  starting transfers between devices: 253 us -> 69.7 us
  loops' own time: 105 us -> 0 us
  local copies, waits for them, and re-layouts: 74.3 us -> 11.2 us
  blocking collectives: 0 us -> 50.5 us
  Pallas kernels: 0 us -> 37 us
  matrix products: 17.1 us -> 0 us
  between operations: 14.7 us -> 0.74 us
    psum x1 -> x0, waiting for transfers between devices: 318 us -> none  [local(): total_qkv, total_out = lax.psum((w_grad_qkv, w_grad_out), ('dp', 'seq'))]
    ppermute x32 -> x6, starting transfers between devices: 253 us -> 48.2 us  [the longest x4 41.1 us: shift(): lax.ppermute(x, 'x', [(i, i + by) for i in range(count) if 0 <= i + by <...]
    ppermute x32 -> x6, waiting for transfers between devices: 154 us -> 22.4 us  [the longest x4 17.8 us: shift(): lax.ppermute(x, 'x', [(i, i + by) for i in range(count) if 0 <= i + by <...]
    another operation x36 -> x0, loops' own time: 105 us -> none  [the longest x1 54.3 us: block_grads(): lax.scan(grad_step, jnp.zeros((tok_rows, head_count, head_size), jnp.floa...]
    all_to_all x0 -> x3, blocking collectives: none -> 50.5 us  [the longest x2 28.3 us: spread(): lax.all_to_all(jnp.broadcast_to(x[None], (count,) + x.shape), axes, 0, 0,...]
    pallas_call x0 -> x4, Pallas kernels: none -> 37 us  [the longest x1 33.4 us: attention(): pl.pallas_call(attention_kernel, out_shape=(jax.ShapeDtypeStruct(own.shap...]
    all_to_all x0 -> x4, starting transfers between devices: none -> 21.5 us  [exchange(): return lax.all_to_all(x, heads_axes, 0, 0, tiled=True)]
    slice x34 -> x1, local copies, waits for them, and re-layouts: 22.8 us -> 1.96 us  [local(): return (grad_in, total[:, :joint_width], total[:, joint_width:])]
  transfers between devices with their start and end apart: 33 -> 10, of which waited for: 15 -> 9; matrix products, arithmetic and copies ran while one was open for 1% -> 1% of each run, Pallas kernels for 0% -> 1%
where the time goes in v1:
time: 209 us
  starting transfers between devices  69.7 us (33%)
  blocking collectives  50.5 us (24%)
  Pallas kernels  37 us (18%)
  waiting for transfers between devices  35.7 us (17%)
  local copies, waits for them, and re-layouts  11.2 us (5%)
  other arithmetic  4.34 us (2%)
    ppermute x4, starting transfers between devices, shift(): lax.ppermute(x, 'x', [(i, i + by) for i in range(count) if 0 <= i + by <...  41.1 us
    pallas_call x1, Pallas kernels, attention(): pl.pallas_call(attention_kernel, out_shape=(jax.ShapeDtypeStruct(own.shap...  33.4 us
    all_to_all x2, blocking collectives, spread(): lax.all_to_all(jnp.broadcast_to(x[None], (count,) + x.shape), axes, 0, 0,...  28.3 us
    all_to_all x1, blocking collectives, local(): lax.all_to_all(part, seq_axes, 0, 0, tiled=True).astype(F32)  22.2 us
    all_to_all x4, starting transfers between devices, exchange(): return lax.all_to_all(x, heads_axes, 0, 0, tiled=True)  21.5 us
    ppermute x4, waiting for transfers between devices, shift(): lax.ppermute(x, 'x', [(i, i + by) for i in range(count) if 0 <= i + by <...  17.8 us
    all_to_all x4, waiting for transfers between devices, exchange(): return lax.all_to_all(x, heads_axes, 0, 0, tiled=True)  13.3 us
    unnamed x28, local copies, waits for them, and re-layouts  9.07 us
  transfers between devices with their start and end apart: 10, of which 9 were waited for; matrix products, arithmetic and copies ran while one was open for 1% of the time, Pallas kernels for 1%

profile of v1, /device:TPU:1, one launch (start us, length us, event | category | flops | bytes accessed | tf_op | source)
XLA Modules:
  0.0 209.0 jit_solution(3885569242733450087)
XLA Ops:
  1.6 0.9 copy-done.8
  2.5 1.0 pack.2
  3.5 6.4 %all-to-all-start = ((bf16[8,256,128]{2,1,0:T(8,128)(2,1)}), bf16[8,256,128]{2,1,0:T(8,128)(2,1)S(1)}, u32[]{:S(2)}, u32[]{:S(2)}) async-start(bf16[8,256,128]{2,1,0:T(8,128)(2,1)} %pack.2), calls=%async_computation | async-start | bytes 1048576 | tf_op jit(solution)/shard_map/all_to_all | solution.py:254
  10.9 1.0 copy-done.3
  11.9 0.9 copy-done.9
  12.8 1.2 pack.3
  14.1 3.7 %all-to-all-done = bf16[8,256,128]{2,1,0:T(8,128)(2,1)S(1)} async-done(((bf16[8,256,128]{2,1,0:T(8,128)(2,1)}), bf16[8,256,128]{2,1,0:T(8,128)(2,1)S(1)}, u32[]{:S(2)}, u32[]{:S(2)}) %all-to-all-start) | async-done | bytes 524320 | tf_op jit(solution)/shard_map/all_to_all | solution.py:254
  17.7 5.2 %all-to-all-start.1 = ((bf16[8,256,128]{2,1,0:T(8,128)(2,1)}), bf16[8,256,128]{2,1,0:T(8,128)(2,1)S(1)}, u32[]{:S(2)}, u32[]{:S(2)}) async-start(bf16[8,256,128]{2,1,0:T(8,128)(2,1)} %pack.3), calls=%async_computation.1 | async-start | bytes 1048576 | tf_op jit(solution)/shard_map/all_to_all | solution.py:254
  22.9 1.3 collective-permute-start.1
  24.2 4.0 %collective-permute-start = (bf16[2048,128]{1,0:T(8,128)(2,1)S(1)}, bf16[2048,128]{1,0:T(8,128)(2,1)S(1)}, u32[]{:S(2)}, u32[]{:S(2)}) collective-permute-start(bf16[2048,128]{1,0:T(8,128)(2,1)S(1)} %bitcast.11), channel_id=1, source_target_pairs={{0,8},{8,16},{16,24},{1,9},{9,17},{17,25},{2,10},{10,18},{18,26},{... | collective-permute-start | bytes 1572872 | tf_op jit(solution)/shard_map/ppermute | solution.py:243
  28.2 2.5 %all-to-all-done.1 = bf16[8,256,128]{2,1,0:T(8,128)(2,1)S(1)} async-done(((bf16[8,256,128]{2,1,0:T(8,128)(2,1)}), bf16[8,256,128]{2,1,0:T(8,128)(2,1)S(1)}, u32[]{:S(2)}, u32[]{:S(2)}) %all-to-all-start.1) | async-done | bytes 524320 | tf_op jit(solution)/shard_map/all_to_all | solution.py:254
  30.7 6.4 %collective-permute-done.1.next_ref = bf16[2048,128]{1,0:T(8,128)(2,1)S(1)} collective-permute-done((bf16[2048,128]{1,0:T(8,128)(2,1)S(1)}, bf16[2048,128]{1,0:T(8,128)(2,1)S(1)}, u32[]{:S(2)}, u32[]{:S(2)}) %collective-permute-start.1) | collective-permute-done | bytes 524320 | tf_op jit(solution)/shard_map/ppermute | solution.py:243
  38.9 1.0 copy-done.6
  39.9 33.4 %attention.1 = (bf16[2048,128]{1,0:T(8,128)(2,1)}, bf16[8,256,128]{2,1,0:T(8,128)(2,1)S(1)}, bf16[8,256,128]{2,1,0:T(8,128)(2,1)S(1)}, bf16[8,256,128]{2,1,0:T(8,128)(2,1)S(1)}) custom-call(s32[1,32]{1,0:T(1,128)S(1)} %copy-done.11, s32[1]{0:T(128)} %bitcast.1.place_ref, bf16[2048,128]{1,0:T(8,128)(2,1)S(1)} %bitcast.12, bf16[2048,128]{1,0:T(8,128)(2,1)S(1)} %copy-done.6, ...), custom_call_target="tpu_custom_call" | custom-call | tf_op jit(solution)/shard_map/attention/pallas_call | solution.py:170
  75.7 5.1 %all-to-all-start.2 = ((bf16[8,256,128]{2,1,0:T(8,128)(2,1)}), bf16[8,256,128]{2,1,0:T(8,128)(2,1)S(1)}, u32[]{:S(2)}, u32[]{:S(2)}) async-start(bf16[8,256,128]{2,1,0:T(8,128)(2,1)} %bitcast.4), calls=%async_computation.2 | async-start | bytes 1048576 | tf_op jit(solution)/shard_map/all_to_all | solution.py:254
  80.8 1.3 collective-permute-start.2
  82.1 34.5 %collective-permute-start.3 = (bf16[8,256,128]{2,1,0:T(8,128)(2,1)}, bf16[8,256,128]{2,1,0:T(8,128)(2,1)S(1)}, u32[]{:S(2)}, u32[]{:S(2)}) collective-permute-start(bf16[8,256,128]{2,1,0:T(8,128)(2,1)} %copy-done.12), channel_id=1, source_target_pairs={{0,8},{8,16},{16,24},{1,9},{9,17},{17,25},{2,10},{10,18},{18,26},{... | collective-permute-start | bytes 1572872 | tf_op jit(solution)/shard_map/ppermute | solution.py:243
  116.6 9.5 %collective-permute-done.2 = bf16[8,256,128]{2,1,0:T(8,128)(2,1)S(1)} collective-permute-done((bf16[8,256,128]{2,1,0:T(8,128)(2,1)}, bf16[8,256,128]{2,1,0:T(8,128)(2,1)S(1)}, u32[]{:S(2)}, u32[]{:S(2)}) %collective-permute-start.2) | collective-permute-done | bytes 524320 | tf_op jit(solution)/shard_map/ppermute | solution.py:243
  126.1 1.0 collective-permute-done.3
  127.1 2.0 add_convert_fusion.1
  129.1 4.9 %all-to-all-start.3 = ((bf16[8,256,128]{2,1,0:T(8,128)(2,1)}), bf16[8,256,128]{2,1,0:T(8,128)(2,1)S(1)}, u32[]{:S(2)}, u32[]{:S(2)}) async-start(bf16[8,256,128]{2,1,0:T(8,128)(2,1)} %add_convert_fusion.1), calls=%async_computation.3 | async-start | bytes 1048576 | tf_op jit(solution)/shard_map/all_to_all | solution.py:254
  134.0 7.1 %all-to-all-done.3.kv_ref = bf16[8,256,128]{2,1,0:T(8,128)(2,1)S(1)} async-done(((bf16[8,256,128]{2,1,0:T(8,128)(2,1)}), bf16[8,256,128]{2,1,0:T(8,128)(2,1)S(1)}, u32[]{:S(2)}, u32[]{:S(2)}) %all-to-all-start.3) | async-done | bytes 524320 | tf_op jit(solution)/shard_map/all_to_all | solution.py:254
  141.1 1.3 finish.1
  142.4 3.6 %collective-permute-start.4 = (bf16[256,2048]{1,0:T(8,128)(2,1)S(1)}, bf16[256,2048]{1,0:T(8,128)(2,1)S(1)}, u32[]{:S(2)}, u32[]{:S(2)}) collective-permute-start(bf16[256,2048]{1,0:T(8,128)(2,1)S(1)} %get-tuple-element.16), channel_id=1, source_target_pairs={{0,32},{32,0},{1,33},{33,1},{2,34},{34,2},{3,35},{35,3},{4,36},{36... | collective-permute-start | bytes 3145736 | tf_op jit(solution)/shard_map/ppermute | solution.py:267
  146.1 2.3 %collective-permute-done.4 = bf16[256,2048]{1,0:T(8,128)(2,1)S(1)} collective-permute-done((bf16[256,2048]{1,0:T(8,128)(2,1)S(1)}, bf16[256,2048]{1,0:T(8,128)(2,1)S(1)}, u32[]{:S(2)}, u32[]{:S(2)}) %collective-permute-start.4) | collective-permute-done | bytes 1048608 | tf_op jit(solution)/shard_map/ppermute | solution.py:267
  148.7 22.2 %all_to_all.35 = bf16[32,8,2048]{2,1,0:T(8,128)(2,1)S(1)} all-to-all(bf16[32,8,2048]{2,1,0:T(8,128)(2,1)S(1)} %fusion), channel_id=1, replica_groups=mesh['zh'=4,'c'=2,'x'=4,'zl'=2,'y'=4] {'x','zl','y'}, dimensions={0} | all-to-all | bytes 2097152 | tf_op jit(solution)/shard_map/all_to_all | solution.py:271
  171.1 9.6 %all_to_all.36 = bf16[4,8,2048]{2,1,0:T(8,128)(2,1)S(1)} all-to-all(bf16[4,8,2048]{2,1,0:T(8,128)(2,1)S(1)} %broadcast_in_dim.4), channel_id=1, replica_groups=mesh['zh'=4,'c'=2,'x'=4,'zl'=2,'y'=4] {'zh'}, dimensions={0} | all-to-all | bytes 262144 | tf_op jit(solution)/shard_map/all_to_all | solution.py:238
  180.9 18.6 %all_to_all.37 = bf16[32,8,2048]{2,1,0:T(8,128)(2,1)S(1)} all-to-all(bf16[32,8,2048]{2,1,0:T(8,128)(2,1)S(1)} %broadcast_in_dim.5), channel_id=1, replica_groups=mesh['zh'=4,'c'=2,'x'=4,'zl'=2,'y'=4] {'x','zl','y'}, dimensions={0} | all-to-all | bytes 2097152 | tf_op jit(solution)/shard_map/all_to_all | solution.py:238
  199.5 3.5 %collective-permute-start.5 = (bf16[256,2048]{1,0:T(8,128)(2,1)S(1)}, bf16[256,2048]{1,0:T(8,128)(2,1)S(1)}, u32[]{:S(2)}, u32[]{:S(2)}) collective-permute-start(bf16[256,2048]{1,0:T(8,128)(2,1)S(1)} %bitcast.14), channel_id=1, source_target_pairs={{0,32},{32,0},{1,33},{33,1},{2,34},{34,2},{3,35},{35,3},{4,36},{36... | collective-permute-start | bytes 3145736 | tf_op jit(solution)/shard_map/ppermute | solution.py:275
  203.0 2.3 %collective-permute-done.5 = bf16[256,2048]{1,0:T(8,128)(2,1)S(1)} collective-permute-done((bf16[256,2048]{1,0:T(8,128)(2,1)S(1)}, bf16[256,2048]{1,0:T(8,128)(2,1)S(1)}, u32[]{:S(2)}, u32[]{:S(2)}) %collective-permute-start.5) | collective-permute-done | bytes 1048608 | tf_op jit(solution)/shard_map/ppermute | solution.py:275
  205.5 1.1 maximum_convert_fusion.1
  207.1 2.0 slice.8
  (33 shorter events, 7.3 us)
Async XLA Ops:
  0.6 1.0 copy-start.7
  1.6 0.9 copy-start.8
  2.5 36.3 %copy-start.11 = (s32[1,32]{1,0:T(1,128)S(1)}, s32[1,32]{1,0:T(1,128)}, u32[]{:S(2)}) copy-start(s32[1,32]{1,0:T(1,128)} %tiles_ref.1) | copy-start | bytes 388
  3.5 14.2 %all-to-all-start = ((bf16[8,256,128]{2,1,0:T(8,128)(2,1)}), bf16[8,256,128]{2,1,0:T(8,128)(2,1)S(1)}, u32[]{:S(2)}, u32[]{:S(2)}) async-start(bf16[8,256,128]{2,1,0:T(8,128)(2,1)} %pack.2), calls=%async_computation | async-start | bytes 1048576 | tf_op jit(solution)/shard_map/all_to_all | solution.py:254
  9.9 0.9 copy-start.1
  10.9 1.0 copy-start.3
  11.9 0.9 copy-start.9
  17.7 13.0 %all-to-all-start.1 = ((bf16[8,256,128]{2,1,0:T(8,128)(2,1)}), bf16[8,256,128]{2,1,0:T(8,128)(2,1)S(1)}, u32[]{:S(2)}, u32[]{:S(2)}) async-start(bf16[8,256,128]{2,1,0:T(8,128)(2,1)} %pack.3), calls=%async_computation.1 | async-start | bytes 1048576 | tf_op jit(solution)/shard_map/all_to_all | solution.py:254
  22.9 14.2 %collective-permute-start.1 = (bf16[2048,128]{1,0:T(8,128)(2,1)S(1)}, bf16[2048,128]{1,0:T(8,128)(2,1)S(1)}, u32[]{:S(2)}, u32[]{:S(2)}) collective-permute-start(bf16[2048,128]{1,0:T(8,128)(2,1)S(1)} %bitcast.10), channel_id=1, source_target_pairs={{8,0},{16,8},{24,16},{9,1},{17,9},{25,17},{10,2},{18,10},{26,18},{... | collective-permute-start | bytes 1572872 | tf_op jit(solution)/shard_map/ppermute | solution.py:243
  24.2 13.9 %collective-permute-start = (bf16[2048,128]{1,0:T(8,128)(2,1)S(1)}, bf16[2048,128]{1,0:T(8,128)(2,1)S(1)}, u32[]{:S(2)}, u32[]{:S(2)}) collective-permute-start(bf16[2048,128]{1,0:T(8,128)(2,1)S(1)} %bitcast.11), channel_id=1, source_target_pairs={{0,8},{8,16},{16,24},{1,9},{9,17},{17,25},{2,10},{10,18},{18,26},{... | collective-permute-start | bytes 1572872 | tf_op jit(solution)/shard_map/ppermute | solution.py:243
  38.1 0.8 copy-start.5
  38.8 1.0 copy-start.6
  39.9 101.2 %copy-start = (bf16[512,1536]{1,0:T(8,128)(2,1)S(1)}, bf16[512,1536]{1,0:T(8,128)(2,1)}, u32[]{:S(2)}) copy-start(bf16[512,1536]{1,0:T(8,128)(2,1)} %wqkv_ref.1) | copy-start | bytes 4718596
  39.9 101.2 %copy-start.2 = (bf16[1,256,512]{2,1,0:T(8,128)(2,1)S(1)}, bf16[1,256,512]{2,1,0:T(8,128)(2,1)}, u32[]{:S(2)}) copy-start(bf16[1,256,512]{2,1,0:T(8,128)(2,1)} %gout_ref.1) | copy-start | bytes 786436
  73.3 0.8 copy-start.4
  74.1 0.8 copy-start.12
  74.9 0.8 copy-start.13
  75.7 65.4 %copy-start.10 = (bf16[1,256,512]{2,1,0:T(8,128)(2,1)S(1)}, bf16[1,256,512]{2,1,0:T(8,128)(2,1)}, u32[]{:S(2)}) copy-start(bf16[1,256,512]{2,1,0:T(8,128)(2,1)} %normed_ref.1) | copy-start | bytes 786436
  75.7 53.4 %all-to-all-start.2 = ((bf16[8,256,128]{2,1,0:T(8,128)(2,1)}), bf16[8,256,128]{2,1,0:T(8,128)(2,1)S(1)}, u32[]{:S(2)}, u32[]{:S(2)}) async-start(bf16[8,256,128]{2,1,0:T(8,128)(2,1)} %bitcast.4), calls=%async_computation.2 | async-start | bytes 1048576 | tf_op jit(solution)/shard_map/all_to_all | solution.py:254
  80.8 45.3 %collective-permute-start.2 = (bf16[8,256,128]{2,1,0:T(8,128)(2,1)}, bf16[8,256,128]{2,1,0:T(8,128)(2,1)S(1)}, u32[]{:S(2)}, u32[]{:S(2)}) collective-permute-start(bf16[8,256,128]{2,1,0:T(8,128)(2,1)} %copy-done.13), channel_id=1, source_target_pairs={{8,0},{16,8},{24,16},{9,1},{17,9},{25,17},{10,2},{18,10},{26,18},{... | collective-permute-start | bytes 1572872 | tf_op jit(solution)/shard_map/ppermute | solution.py:243
  82.1 45.0 %collective-permute-start.3 = (bf16[8,256,128]{2,1,0:T(8,128)(2,1)}, bf16[8,256,128]{2,1,0:T(8,128)(2,1)S(1)}, u32[]{:S(2)}, u32[]{:S(2)}) collective-permute-start(bf16[8,256,128]{2,1,0:T(8,128)(2,1)} %copy-done.12), channel_id=1, source_target_pairs={{0,8},{8,16},{16,24},{1,9},{9,17},{17,25},{2,10},{10,18},{18,26},{... | collective-permute-start | bytes 1572872 | tf_op jit(solution)/shard_map/ppermute | solution.py:243
  129.1 12.0 %all-to-all-start.3 = ((bf16[8,256,128]{2,1,0:T(8,128)(2,1)}), bf16[8,256,128]{2,1,0:T(8,128)(2,1)S(1)}, u32[]{:S(2)}, u32[]{:S(2)}) async-start(bf16[8,256,128]{2,1,0:T(8,128)(2,1)} %add_convert_fusion.1), calls=%async_computation.3 | async-start | bytes 1048576 | tf_op jit(solution)/shard_map/all_to_all | solution.py:254
  142.4 5.9 %collective-permute-start.4 = (bf16[256,2048]{1,0:T(8,128)(2,1)S(1)}, bf16[256,2048]{1,0:T(8,128)(2,1)S(1)}, u32[]{:S(2)}, u32[]{:S(2)}) collective-permute-start(bf16[256,2048]{1,0:T(8,128)(2,1)S(1)} %get-tuple-element.16), channel_id=1, source_target_pairs={{0,32},{32,0},{1,33},{33,1},{2,34},{34,2},{3,35},{35,3},{4,36},{36... | collective-permute-start | bytes 3145736 | tf_op jit(solution)/shard_map/ppermute | solution.py:267
  199.5 5.8 %collective-permute-start.5 = (bf16[256,2048]{1,0:T(8,128)(2,1)S(1)}, bf16[256,2048]{1,0:T(8,128)(2,1)S(1)}, u32[]{:S(2)}, u32[]{:S(2)}) collective-permute-start(bf16[256,2048]{1,0:T(8,128)(2,1)S(1)} %bitcast.14), channel_id=1, source_target_pairs={{0,32},{32,0},{1,33},{33,1},{2,34},{34,2},{3,35},{35,3},{4,36},{36... | collective-permute-start | bytes 3145736 | tf_op jit(solution)/shard_map/ppermute | solution.py:275

commit v2 on v1

--- a/solution.py
+++ b/solution.py
@@ -11,6 +11,8 @@
 TILE = 32
 TOK = 256
 SCENES = 32
+STEPS = (8, 4, 2, 1)
+QUERIES = 512
 BARRED = 16384.0
 F32 = jnp.float32
 BF16 = jnp.bfloat16
@@ -31,6 +33,10 @@
     return pl.BlockSpec(memory_space=pltpu.SMEM)
 
 
+def anywhere():
+    return pl.BlockSpec(memory_space=pl.ANY)
+
+
 def dot(a, b, dims=(((1,), (0,)), ((), ()))):
     return lax.dot_general(a, b, dims, preferred_element_type=F32)
 
@@ -51,13 +57,22 @@
 
 
 def attention_kernel(
-    tiles_ref, place_ref, own_ref, prev_ref, next_ref, qd_ref,
-    aq_ref, kv_own_ref, kv_prev_ref, kv_next_ref,
+    tiles_ref, place_ref, own_hbm, prev_hbm, next_hbm, qd_hbm,
+    aq_hbm, kv_own_hbm, kv_prev_hbm, kv_next_hbm,
+    own_ref, prev_ref, next_ref, qd_ref, aq_ref, kv_ref, came, left,
     packed, keys, turned, scores, weights, totals,
 ):
+    arrivals = [
+        pltpu.make_async_copy(source, target, came.at[n])
+        for n, (source, target) in enumerate(
+            ((own_hbm, own_ref), (qd_hbm, qd_ref), (prev_hbm, prev_ref), (next_hbm, next_ref))
+        )
+    ]
+    for copy in arrivals:
+        copy.start()
     quarter = own_ref.shape[0]
     per_quarter = quarter // TOK
-    blocks = 3 * per_quarter
+    query_blocks = quarter // QUERIES
     first_query = place_ref[0] * quarter
     first_key = first_query - quarter
 
@@ -71,9 +86,9 @@
         starts = jnp.where(mine, start, starts)
         ends = jnp.where(mine, end, ends)
         new_lows, new_highs = [], []
-        for i in range(per_quarter):
-            head = first_query + i * TOK
-            tail = head + TOK - 1
+        for i in range(query_blocks):
+            head = first_query + i * QUERIES
+            tail = head + QUERIES - 1
             new_lows.append(jnp.where(jnp.logical_and(start <= head, head < end), start, lows[i]))
             new_highs.append(jnp.where(jnp.logical_and(start <= tail, tail < end), end, highs[i]))
         return end, starts, ends, tuple(new_lows), tuple(new_highs)
@@ -81,13 +96,15 @@
     zero = jnp.int32(0)
     nowhere = jnp.full((1, 128), 2**30, jnp.int32)
     _, starts, ends, lows, highs = lax.fori_loop(
-        0, SCENES, read_scenes, (zero, nowhere, nowhere, (zero,) * per_quarter, (zero,) * per_quarter)
+        0, SCENES, read_scenes, (zero, nowhere, nowhere, (zero,) * query_blocks, (zero,) * query_blocks)
     )
     firsts = [(x - first_key) // TOK for x in lows]
     lasts = [(x - first_key + TOK - 1) // TOK for x in highs]
 
     scene_lane = jnp.logical_and(lane >= HEAD, lane < HEAD + SCENES)
     rows = lax.broadcasted_iota(jnp.int32, (TOK, 1), 0)
+
+    query_rows = lax.broadcasted_iota(jnp.int32, (QUERIES, 1), 0)
 
     def prepare(source_ref, base):
         def body(j, _):
@@ -101,66 +118,89 @@
             return 0
         return body
 
+    totals[...] = jnp.zeros_like(totals)
+    for copy in arrivals:
+        copy.wait()
     begin, finish = firsts[0], lasts[-1]
     for part, source in enumerate((prev_ref, own_ref, next_ref)):
         base = part * per_quarter
         lax.fori_loop(
             jnp.maximum(begin, base), jnp.minimum(finish, base + per_quarter), prepare(source, base), 0
         )
-    totals[...] = jnp.zeros_like(totals)
-
-    for i in range(per_quarter):
-        span = slice(i * TOK, (i + 1) * TOK)
+
+    def sweep(first, last, body, carry):
+        for step in STEPS:
+            groups = (last - first) // step
+
+            def many(t, c, first=first, step=step):
+                for u in range(step):
+                    c = body(first + t * step + u, c)
+                return c
+
+            carry = lax.fori_loop(0, groups, many, carry)
+            first = first + groups * step
+        return carry
+
+    leaving = []
+    for i in range(query_blocks):
+        span = slice(i * QUERIES, (i + 1) * QUERIES)
         qd = qd_ref[span, :]
-        position = first_query + i * TOK + rows
+        position = first_query + i * QUERIES + query_rows
         same = jnp.logical_and(position >= starts, position < ends)
         other = jnp.where(jnp.logical_and(scene_lane, jnp.logical_not(same)), -BARRED, 0.0)
-        query = jnp.where(low, qd.astype(F32) * HEAD**-0.5, other).astype(BF16)
+        scaled = qd.astype(F32) * HEAD**-0.5
+        query = jnp.where(low, scaled, other).T.astype(BF16)
         nil = jnp.zeros_like(qd)
-        only_q = jnp.where(low, (qd.astype(F32) * HEAD**-0.5).astype(BF16), nil)
+        only_q = jnp.where(low, scaled.astype(BF16), nil)
         only_d = jnp.where(low, nil, qd)
         pair = jnp.concatenate([only_q, only_d], axis=0)
+        grad = only_d.T
 
         def first_pass(j, top):
-            s = dot(keys[j], query, NT)
+            s = dot(keys[j], query)
             scores[j] = s
-            return jnp.maximum(top, jnp.max(s.reshape(TOK // 8, 8, TOK), axis=0))
-
-        top = lax.fori_loop(firsts[i], lasts[i], first_pass, jnp.full((8, TOK), -1e30, F32))
+            return jnp.maximum(top, jnp.max(s.reshape(TOK // 8, 8, QUERIES), axis=0))
+
+        top = sweep(firsts[i], lasts[i], first_pass, jnp.full((8, QUERIES), -1e30, F32))
         top = jnp.max(top, axis=0, keepdims=True)
 
         def second_pass(j, carry):
             total, attended = carry
             p = jnp.exp(scores[j] - top)
-            total = total + jnp.sum(p.reshape(TOK // 8, 8, TOK), axis=0)
+            total = total + jnp.sum(p.reshape(TOK // 8, 8, QUERIES), axis=0)
             p = p.astype(BF16)
             weights[j] = p
             attended = attended + dot(turned[j, HEAD:, :], p)
             return total, attended
 
-        total, attended = lax.fori_loop(
-            firsts[i], lasts[i], second_pass, (jnp.zeros((8, TOK), F32), jnp.zeros((HEAD, TOK), F32))
+        total, attended = sweep(
+            firsts[i], lasts[i], second_pass, (jnp.zeros((8, QUERIES), F32), jnp.zeros((HEAD, QUERIES), F32))
         )
         share = 1.0 / jnp.sum(total, axis=0, keepdims=True)
         attended = (attended * share).astype(BF16).astype(F32)
-        grad_turned = qd.T[HEAD:, :].astype(F32)
-        row_dot = jnp.sum(attended * grad_turned, axis=0, keepdims=True)
+        row_dot = jnp.sum(attended * grad[HEAD:, :].astype(F32), axis=0, keepdims=True)
 
         def third_pass(j, grad_query):
-            grad_probs = dot(packed[j], only_d, NT)
+            grad_probs = dot(packed[j], grad)
             probs = weights[j].astype(F32) * share
             grad_scores = (probs * (grad_probs - row_dot)).astype(BF16)
             both = jnp.concatenate([grad_scores, probs.astype(BF16)], axis=1)
             totals[j] += dot(both, pair)
             return grad_query + dot(turned[j, :HEAD, :], grad_scores)
 
-        grad_query = lax.fori_loop(firsts[i], lasts[i], third_pass, jnp.zeros((HEAD, TOK), F32))
+        grad_query = sweep(firsts[i], lasts[i], third_pass, jnp.zeros((HEAD, QUERIES), F32))
         out = jnp.concatenate([attended, grad_query * HEAD**-0.5], axis=0)
         aq_ref[span, :] = out.T.astype(BF16)
-
-    for part, out_ref in enumerate((kv_prev_ref, kv_own_ref, kv_next_ref)):
+        leaving.append(pltpu.make_async_copy(aq_ref.at[span], aq_hbm.at[span], left.at[i]))
+        leaving[-1].start()
+
+    for part, out_hbm in enumerate((kv_prev_hbm, kv_own_hbm, kv_next_hbm)):
         for j in range(per_quarter):
-            out_ref[j] = totals[part * per_quarter + j].astype(BF16)
+            kv_ref[part, j] = totals[part * per_quarter + j].astype(BF16)
+        leaving.append(pltpu.make_async_copy(kv_ref.at[part], out_hbm, left.at[query_blocks + part]))
+        leaving[-1].start()
+    for copy in leaving:
+        copy.wait()
 
 
 def attention(scene_tiles, place, own, prev, after, qd):
@@ -170,14 +210,17 @@
     return pl.pallas_call(
         attention_kernel,
         out_shape=(jax.ShapeDtypeStruct(own.shape, BF16), grads, grads, grads),
-        in_specs=[smem(), smem()] + [vmem()] * 4,
-        out_specs=(vmem(),) * 4,
-        scratch_shapes=[
+        in_specs=[smem(), smem()] + [anywhere()] * 4,
+        out_specs=(anywhere(),) * 4,
+        scratch_shapes=[pltpu.VMEM(own.shape, BF16)] * 5 + [
+            pltpu.VMEM((3, quarter // TOK, TOK, 2 * HEAD), BF16),
+            pltpu.SemaphoreType.DMA((4,)),
+            pltpu.SemaphoreType.DMA((quarter // QUERIES + 3,)),
             pltpu.VMEM((blocks, TOK, 2 * HEAD), BF16),
             pltpu.VMEM((blocks, TOK, 2 * HEAD), BF16),
             pltpu.VMEM((blocks, 2 * HEAD, TOK), BF16),
-            pltpu.VMEM((blocks, TOK, TOK), F32),
-            pltpu.VMEM((blocks, TOK, TOK), BF16),
+            pltpu.VMEM((blocks, TOK, QUERIES), F32),
+            pltpu.VMEM((blocks, TOK, QUERIES), BF16),
             pltpu.VMEM((blocks, TOK, 2 * HEAD), F32),
         ],
         compiler_params=params(),
@@ -269,9 +312,11 @@
     rows, columns = part.shape
     part = part.reshape(seq_count, rows // seq_count, columns)
     part = jnp.sum(lax.all_to_all(part, seq_axes, 0, 0, tiled=True).astype(F32), axis=0)
-    part = jnp.sum(spread(part.astype(BF16), ("zh",), lax.axis_size("zh")).astype(F32)
-                   .reshape((-1,) + part.shape), axis=0)
-    mine = spread(part.astype(BF16), seq_axes, seq_count).reshape(rows, columns)
+    part = part.astype(BF16)
+    for step in (1, 2):
+        partner = [(i, i ^ step) for i in range(lax.axis_size("zh"))]
+        part = (part.astype(F32) + lax.ppermute(part, "zh", partner).astype(F32)).astype(BF16)
+    mine = spread(part, seq_axes, seq_count).reshape(rows, columns)
     other = lax.ppermute(mine, "c", swap)
     first = core[0] == 0
     total = jnp.concatenate([jnp.where(first, mine, other), jnp.where(first, other, mine)], axis=0)

time: 209 us -> 188 us (0.90); the launches traced: 209 us -> 185 us
  starting transfers between devices: 69.7 us -> 52.7 us
  Pallas kernels: 37 us -> 32.2 us
  blocking collectives: 50.5 us -> 45.8 us
  waiting for transfers between devices: 35.7 us -> 37.8 us
    ppermute x4, starting transfers between devices: 41.1 us -> 17.5 us  [shift(): lax.ppermute(x, 'x', [(i, i + by) for i in range(count) if 0 <= i + by <...]
    all_to_all x2 -> x1, blocking collectives: 28.3 us -> 18.2 us  [spread(): lax.all_to_all(jnp.broadcast_to(x[None], (count,) + x.shape), axes, 0, 0,...]
    ppermute x0 -> x2, starting transfers between devices: none -> 9.01 us  [local(): lax.ppermute(part, 'zh', partner).astype(F32)]
    all_to_all x1, blocking collectives: 22.2 us -> 27.7 us  [local(): lax.all_to_all(part, seq_axes, 0, 0, tiled=True).astype(F32)]
    ppermute x0 -> x2, waiting for transfers between devices: none -> 5.31 us  [local(): lax.ppermute(part, 'zh', partner).astype(F32)]
    pallas_call x1, Pallas kernels: 33.4 us -> 28.6 us  [attention(): pl.pallas_call(attention_kernel, out_shape=(jax.ShapeDtypeStruct(own.shap...]
    ppermute x1, starting transfers between devices: 3.61 us -> 0.01 us  [local(): came = lax.ppermute(send, 'c', swap)]
    ppermute x4, waiting for transfers between devices: 17.8 us -> 14.3 us  [shift(): lax.ppermute(x, 'x', [(i, i + by) for i in range(count) if 0 <= i + by <...]
  transfers between devices with their start and end apart: 10 -> 12, of which waited for: 9 -> 11; matrix products, arithmetic and copies ran while one was open for 1% -> 1% of each run, Pallas kernels for 1% -> 1%
where the time goes in v2:
time: 188 us; the launch traced here: 185 us
  starting transfers between devices  52.7 us (28%)
  blocking collectives  45.8 us (24%)
  waiting for transfers between devices  37.8 us (20%)
  Pallas kernels  32.2 us (17%)
  local copies, waits for them, and re-layouts  11.2 us (6%)
  other arithmetic  4.34 us (2%)
    pallas_call x1, Pallas kernels, attention(): pl.pallas_call(attention_kernel, out_shape=(jax.ShapeDtypeStruct(own.shap...  28.6 us
    all_to_all x1, blocking collectives, local(): lax.all_to_all(part, seq_axes, 0, 0, tiled=True).astype(F32)  27.7 us
    all_to_all x4, starting transfers between devices, exchange(): return lax.all_to_all(x, heads_axes, 0, 0, tiled=True)  22.1 us
    all_to_all x1, blocking collectives, spread(): lax.all_to_all(jnp.broadcast_to(x[None], (count,) + x.shape), axes, 0, 0,...  18.2 us
    ppermute x4, starting transfers between devices, shift(): lax.ppermute(x, 'x', [(i, i + by) for i in range(count) if 0 <= i + by <...  17.5 us
    ppermute x4, waiting for transfers between devices, shift(): lax.ppermute(x, 'x', [(i, i + by) for i in range(count) if 0 <= i + by <...  14.3 us
    all_to_all x4, waiting for transfers between devices, exchange(): return lax.all_to_all(x, heads_axes, 0, 0, tiled=True)  13.3 us
    unnamed x28, local copies, waits for them, and re-layouts  9.09 us
  transfers between devices with their start and end apart: 12, of which 11 were waited for; matrix products, arithmetic and copies ran while one was open for 1% of the time, Pallas kernels for 1%

profile of v2, /device:TPU:1, one launch (start us, length us, event | category | flops | bytes accessed | tf_op | source)
XLA Modules:
  0.0 185.0 jit_solution(15632770592894449236)
XLA Ops:
  1.6 0.9 copy-done.8
  2.5 1.0 pack.2
  3.5 6.4 %all-to-all-start = ((bf16[8,256,128]{2,1,0:T(8,128)(2,1)}), bf16[8,256,128]{2,1,0:T(8,128)(2,1)S(1)}, u32[]{:S(2)}, u32[]{:S(2)}) async-start(bf16[8,256,128]{2,1,0:T(8,128)(2,1)} %pack.2), calls=%async_computation | async-start | bytes 1048576 | tf_op jit(solution)/shard_map/all_to_all | solution.py:297
  10.9 1.0 copy-done.3
  12.8 1.2 pack.3
  14.1 3.7 %all-to-all-done = bf16[8,256,128]{2,1,0:T(8,128)(2,1)S(1)} async-done(((bf16[8,256,128]{2,1,0:T(8,128)(2,1)}), bf16[8,256,128]{2,1,0:T(8,128)(2,1)S(1)}, u32[]{:S(2)}, u32[]{:S(2)}) %all-to-all-start) | async-done | bytes 524320 | tf_op jit(solution)/shard_map/all_to_all | solution.py:297
  17.7 5.2 %all-to-all-start.1 = ((bf16[8,256,128]{2,1,0:T(8,128)(2,1)}), bf16[8,256,128]{2,1,0:T(8,128)(2,1)S(1)}, u32[]{:S(2)}, u32[]{:S(2)}) async-start(bf16[8,256,128]{2,1,0:T(8,128)(2,1)} %pack.3), calls=%async_computation.1 | async-start | bytes 1048576 | tf_op jit(solution)/shard_map/all_to_all | solution.py:297
  22.9 1.3 collective-permute-start.1
  24.2 4.0 %collective-permute-start = (bf16[2048,128]{1,0:T(8,128)(2,1)S(1)}, bf16[2048,128]{1,0:T(8,128)(2,1)S(1)}, u32[]{:S(2)}, u32[]{:S(2)}) collective-permute-start(bf16[2048,128]{1,0:T(8,128)(2,1)S(1)} %bitcast.11), channel_id=1, source_target_pairs={{0,8},{8,16},{16,24},{1,9},{9,17},{17,25},{2,10},{10,18},{18,26},{... | collective-permute-start | bytes 1572872 | tf_op jit(solution)/shard_map/ppermute | solution.py:286
  28.2 2.5 %all-to-all-done.1 = bf16[8,256,128]{2,1,0:T(8,128)(2,1)S(1)} async-done(((bf16[8,256,128]{2,1,0:T(8,128)(2,1)}), bf16[8,256,128]{2,1,0:T(8,128)(2,1)S(1)}, u32[]{:S(2)}, u32[]{:S(2)}) %all-to-all-start.1) | async-done | bytes 524320 | tf_op jit(solution)/shard_map/all_to_all | solution.py:297
  30.7 6.4 %collective-permute-done.1.next_hbm = bf16[2048,128]{1,0:T(8,128)(2,1)S(1)} collective-permute-done((bf16[2048,128]{1,0:T(8,128)(2,1)S(1)}, bf16[2048,128]{1,0:T(8,128)(2,1)S(1)}, u32[]{:S(2)}, u32[]{:S(2)}) %collective-permute-start.1) | collective-permute-done | bytes 524320 | tf_op jit(solution)/shard_map/ppermute | solution.py:286
  38.9 1.0 copy-done.6
  39.9 28.6 %attention.1 = (bf16[2048,128]{1,0:T(8,128)(2,1)}, bf16[8,256,128]{2,1,0:T(8,128)(2,1)S(1)}, bf16[8,256,128]{2,1,0:T(8,128)(2,1)S(1)}, bf16[8,256,128]{2,1,0:T(8,128)(2,1)S(1)}) custom-call(s32[1,32]{1,0:T(1,128)S(1)} %copy-done.11, s32[1]{0:T(128)} %bitcast.1.place_ref, bf16[2048,128]{1,0:T(8,128)(2,1)S(1)} %bitcast.12, bf16[2048,128]{1,0:T(8,128)(2,1)S(1)} %copy-done.6, ...), custom_call_target="tpu_custom_call" | custom-call | tf_op jit(solution)/shard_map/attention/pallas_call | solution.py:210
  71.0 5.1 %all-to-all-start.2 = ((bf16[8,256,128]{2,1,0:T(8,128)(2,1)}), bf16[8,256,128]{2,1,0:T(8,128)(2,1)S(1)}, u32[]{:S(2)}, u32[]{:S(2)}) async-start(bf16[8,256,128]{2,1,0:T(8,128)(2,1)} %bitcast.4), calls=%async_computation.2 | async-start | bytes 1048576 | tf_op jit(solution)/shard_map/all_to_all | solution.py:297
  76.0 1.3 collective-permute-start.2
  77.3 10.9 %collective-permute-start.3 = (bf16[8,256,128]{2,1,0:T(8,128)(2,1)}, bf16[8,256,128]{2,1,0:T(8,128)(2,1)S(1)}, u32[]{:S(2)}, u32[]{:S(2)}) collective-permute-start(bf16[8,256,128]{2,1,0:T(8,128)(2,1)} %copy-done.12), channel_id=1, source_target_pairs={{0,8},{8,16},{16,24},{1,9},{9,17},{17,25},{2,10},{10,18},{18,26},{... | collective-permute-start | bytes 1572872 | tf_op jit(solution)/shard_map/ppermute | solution.py:286
  88.2 5.1 %collective-permute-done.2 = bf16[8,256,128]{2,1,0:T(8,128)(2,1)S(1)} collective-permute-done((bf16[8,256,128]{2,1,0:T(8,128)(2,1)}, bf16[8,256,128]{2,1,0:T(8,128)(2,1)S(1)}, u32[]{:S(2)}, u32[]{:S(2)}) %collective-permute-start.2) | collective-permute-done | bytes 524320 | tf_op jit(solution)/shard_map/ppermute | solution.py:286
  93.3 1.9 %collective-permute-done.3 = bf16[8,256,128]{2,1,0:T(8,128)(2,1)S(1)} collective-permute-done((bf16[8,256,128]{2,1,0:T(8,128)(2,1)}, bf16[8,256,128]{2,1,0:T(8,128)(2,1)S(1)}, u32[]{:S(2)}, u32[]{:S(2)}) %collective-permute-start.3) | collective-permute-done | bytes 524320 | tf_op jit(solution)/shard_map/ppermute | solution.py:286
  95.2 2.0 %add_convert_fusion.1 = bf16[8,256,128]{2,1,0:T(8,128)(2,1)} fusion(bf16[8,256,128]{2,1,0:T(8,128)(2,1)S(1)} %collective-permute-done.3, bf16[8,256,128]{2,1,0:T(8,128)(2,1)S(1)} %collective-permute-done.2, bf16[8,256,128]{2,1,0:T(8,128)(2,1)} %copy-done.4), kind=kLoop, calls=%fused_computation.3 | loop fusion | flops 1572864 | bytes 2097152 | tf_op jit(solution)/shard_map/convert_element_type | solution.py:305
  97.2 5.4 %all-to-all-start.3 = ((bf16[8,256,128]{2,1,0:T(8,128)(2,1)}), bf16[8,256,128]{2,1,0:T(8,128)(2,1)S(1)}, u32[]{:S(2)}, u32[]{:S(2)}) async-start(bf16[8,256,128]{2,1,0:T(8,128)(2,1)} %add_convert_fusion.1), calls=%async_computation.3 | async-start | bytes 1048576 | tf_op jit(solution)/shard_map/all_to_all | solution.py:297
  102.7 7.1 %all-to-all-done.3.kv_ref = bf16[8,256,128]{2,1,0:T(8,128)(2,1)S(1)} async-done(((bf16[8,256,128]{2,1,0:T(8,128)(2,1)}), bf16[8,256,128]{2,1,0:T(8,128)(2,1)S(1)}, u32[]{:S(2)}, u32[]{:S(2)}) %all-to-all-start.3) | async-done | bytes 524320 | tf_op jit(solution)/shard_map/all_to_all | solution.py:297
  109.8 1.3 finish.1
  111.1 2.7 %collective-permute-done.4 = bf16[256,2048]{1,0:T(8,128)(2,1)S(1)} collective-permute-done((bf16[256,2048]{1,0:T(8,128)(2,1)S(1)}, bf16[256,2048]{1,0:T(8,128)(2,1)S(1)}, u32[]{:S(2)}, u32[]{:S(2)}) %collective-permute-start.4) | collective-permute-done | bytes 1048608 | tf_op jit(solution)/shard_map/ppermute | solution.py:310
  114.2 27.7 %all_to_all.30 = bf16[32,8,2048]{2,1,0:T(8,128)(2,1)S(1)} all-to-all(bf16[32,8,2048]{2,1,0:T(8,128)(2,1)S(1)} %fusion), channel_id=1, replica_groups=mesh['zh'=4,'c'=2,'x'=4,'zl'=2,'y'=4] {'x','zl','y'}, dimensions={0} | all-to-all | bytes 2097152 | tf_op jit(solution)/shard_map/all_to_all | solution.py:314
  142.1 4.0 %collective-permute-done.5 = bf16[8,2048]{1,0:T(8,128)(2,1)S(1)} collective-permute-done((bf16[8,2048]{1,0:T(8,128)(2,1)S(1)}, bf16[8,2048]{1,0:T(8,128)(2,1)S(1)}, u32[]{:S(2)}, u32[]{:S(2)}) %collective-permute-start.5) | collective-permute-done | bytes 32800 | tf_op jit(solution)/shard_map/ppermute | solution.py:318
  146.1 8.9 %collective-permute-start.6 = (bf16[8,2048]{1,0:T(8,128)(2,1)S(1)}, bf16[8,2048]{1,0:T(8,128)(2,1)S(1)}, u32[]{:S(2)}, u32[]{:S(2)}) collective-permute-start(bf16[8,2048]{1,0:T(8,128)(2,1)S(1)} %add_convert_fusion.3), channel_id=1, source_target_pairs={{0,128},{64,192},{128,0},{192,64},{1,129},{65,193},{129,1},{193,65... | collective-permute-start | bytes 98312 | tf_op jit(solution)/shard_map/ppermute | solution.py:318
  155.1 1.3 collective-permute-done.6
  156.5 18.2 %all_to_all.31 = bf16[32,8,2048]{2,1,0:T(8,128)(2,1)S(1)} all-to-all(bf16[32,8,2048]{2,1,0:T(8,128)(2,1)S(1)} %broadcast_in_dim.2), channel_id=1, replica_groups=mesh['zh'=4,'c'=2,'x'=4,'zl'=2,'y'=4] {'x','zl','y'}, dimensions={0} | all-to-all | bytes 2097152 | tf_op jit(solution)/shard_map/all_to_all | solution.py:281
  174.7 4.2 %collective-permute-start.7 = (bf16[256,2048]{1,0:T(8,128)(2,1)S(1)}, bf16[256,2048]{1,0:T(8,128)(2,1)S(1)}, u32[]{:S(2)}, u32[]{:S(2)}) collective-permute-start(bf16[256,2048]{1,0:T(8,128)(2,1)S(1)} %bitcast.14), channel_id=1, source_target_pairs={{0,32},{32,0},{1,33},{33,1},{2,34},{34,2},{3,35},{35,3},{4,36},{36... | collective-permute-start | bytes 3145736 | tf_op jit(solution)/shard_map/ppermute | solution.py:320
  178.8 2.3 %collective-permute-done.7 = bf16[256,2048]{1,0:T(8,128)(2,1)S(1)} collective-permute-done((bf16[256,2048]{1,0:T(8,128)(2,1)S(1)}, bf16[256,2048]{1,0:T(8,128)(2,1)S(1)}, u32[]{:S(2)}, u32[]{:S(2)}) %collective-permute-start.7) | collective-permute-done | bytes 1048608 | tf_op jit(solution)/shard_map/ppermute | solution.py:320
  181.3 1.1 maximum_convert_fusion.1
  182.9 2.0 %slice.8 = f32[512,1536]{1,0:T(8,128)} slice(f32[512,2048]{1,0:T(8,128)S(1)} %maximum_convert_fusion), slice={[0:512], [0:1536]} | slice | bytes 6291456 | tf_op jit(solution)/shard_map/slice | solution.py:325
  (36 shorter events, 8.4 us)
Async XLA Ops:
  0.6 1.0 copy-start.7
  1.6 0.9 copy-start.8
  2.5 36.3 %copy-start.11 = (s32[1,32]{1,0:T(1,128)S(1)}, s32[1,32]{1,0:T(1,128)}, u32[]{:S(2)}) copy-start(s32[1,32]{1,0:T(1,128)} %tiles_ref.1) | copy-start | bytes 388
  3.5 14.2 %all-to-all-start = ((bf16[8,256,128]{2,1,0:T(8,128)(2,1)}), bf16[8,256,128]{2,1,0:T(8,128)(2,1)S(1)}, u32[]{:S(2)}, u32[]{:S(2)}) async-start(bf16[8,256,128]{2,1,0:T(8,128)(2,1)} %pack.2), calls=%async_computation | async-start | bytes 1048576 | tf_op jit(solution)/shard_map/all_to_all | solution.py:297
  9.9 0.9 copy-start.1
  10.9 1.0 copy-start.3
  11.9 0.9 copy-start.9
  17.7 13.0 %all-to-all-start.1 = ((bf16[8,256,128]{2,1,0:T(8,128)(2,1)}), bf16[8,256,128]{2,1,0:T(8,128)(2,1)S(1)}, u32[]{:S(2)}, u32[]{:S(2)}) async-start(bf16[8,256,128]{2,1,0:T(8,128)(2,1)} %pack.3), calls=%async_computation.1 | async-start | bytes 1048576 | tf_op jit(solution)/shard_map/all_to_all | solution.py:297
  22.9 14.2 %collective-permute-start.1 = (bf16[2048,128]{1,0:T(8,128)(2,1)S(1)}, bf16[2048,128]{1,0:T(8,128)(2,1)S(1)}, u32[]{:S(2)}, u32[]{:S(2)}) collective-permute-start(bf16[2048,128]{1,0:T(8,128)(2,1)S(1)} %bitcast.10), channel_id=1, source_target_pairs={{8,0},{16,8},{24,16},{9,1},{17,9},{25,17},{10,2},{18,10},{26,18},{... | collective-permute-start | bytes 1572872 | tf_op jit(solution)/shard_map/ppermute | solution.py:286
  24.2 13.9 %collective-permute-start = (bf16[2048,128]{1,0:T(8,128)(2,1)S(1)}, bf16[2048,128]{1,0:T(8,128)(2,1)S(1)}, u32[]{:S(2)}, u32[]{:S(2)}) collective-permute-start(bf16[2048,128]{1,0:T(8,128)(2,1)S(1)} %bitcast.11), channel_id=1, source_target_pairs={{0,8},{8,16},{16,24},{1,9},{9,17},{17,25},{2,10},{10,18},{18,26},{... | collective-permute-start | bytes 1572872 | tf_op jit(solution)/shard_map/ppermute | solution.py:286
  38.1 0.8 copy-start.5
  38.8 1.0 copy-start.6
  39.9 69.9 %copy-start = (bf16[512,1536]{1,0:T(8,128)(2,1)S(1)}, bf16[512,1536]{1,0:T(8,128)(2,1)}, u32[]{:S(2)}) copy-start(bf16[512,1536]{1,0:T(8,128)(2,1)} %wqkv_ref.1) | copy-start | bytes 4718596
  39.9 69.9 %copy-start.2 = (bf16[1,256,512]{2,1,0:T(8,128)(2,1)S(1)}, bf16[1,256,512]{2,1,0:T(8,128)(2,1)}, u32[]{:S(2)}) copy-start(bf16[1,256,512]{2,1,0:T(8,128)(2,1)} %gout_ref.1) | copy-start | bytes 786436
  68.5 0.8 copy-start.4
  69.4 0.8 copy-start.12
  70.2 0.8 copy-start.13
  71.0 38.8 %copy-start.10 = (bf16[1,256,512]{2,1,0:T(8,128)(2,1)S(1)}, bf16[1,256,512]{2,1,0:T(8,128)(2,1)}, u32[]{:S(2)}) copy-start(bf16[1,256,512]{2,1,0:T(8,128)(2,1)} %normed_ref.1) | copy-start | bytes 786436
  71.0 26.3 %all-to-all-start.2 = ((bf16[8,256,128]{2,1,0:T(8,128)(2,1)}), bf16[8,256,128]{2,1,0:T(8,128)(2,1)S(1)}, u32[]{:S(2)}, u32[]{:S(2)}) async-start(bf16[8,256,128]{2,1,0:T(8,128)(2,1)} %bitcast.4), calls=%async_computation.2 | async-start | bytes 1048576 | tf_op jit(solution)/shard_map/all_to_all | solution.py:297
  76.0 17.3 %collective-permute-start.2 = (bf16[8,256,128]{2,1,0:T(8,128)(2,1)}, bf16[8,256,128]{2,1,0:T(8,128)(2,1)S(1)}, u32[]{:S(2)}, u32[]{:S(2)}) collective-permute-start(bf16[8,256,128]{2,1,0:T(8,128)(2,1)} %copy-done.13), channel_id=1, source_target_pairs={{8,0},{16,8},{24,16},{9,1},{17,9},{25,17},{10,2},{18,10},{26,18},{... | collective-permute-start | bytes 1572872 | tf_op jit(solution)/shard_map/ppermute | solution.py:286
  77.3 17.9 %collective-permute-start.3 = (bf16[8,256,128]{2,1,0:T(8,128)(2,1)}, bf16[8,256,128]{2,1,0:T(8,128)(2,1)S(1)}, u32[]{:S(2)}, u32[]{:S(2)}) collective-permute-start(bf16[8,256,128]{2,1,0:T(8,128)(2,1)} %copy-done.12), channel_id=1, source_target_pairs={{0,8},{8,16},{16,24},{1,9},{9,17},{17,25},{2,10},{10,18},{18,26},{... | collective-permute-start | bytes 1572872 | tf_op jit(solution)/shard_map/ppermute | solution.py:286
  97.2 12.6 %all-to-all-start.3 = ((bf16[8,256,128]{2,1,0:T(8,128)(2,1)}), bf16[8,256,128]{2,1,0:T(8,128)(2,1)S(1)}, u32[]{:S(2)}, u32[]{:S(2)}) async-start(bf16[8,256,128]{2,1,0:T(8,128)(2,1)} %add_convert_fusion.1), calls=%async_computation.3 | async-start | bytes 1048576 | tf_op jit(solution)/shard_map/all_to_all | solution.py:297
  111.1 2.7 %collective-permute-start.4 = (bf16[256,2048]{1,0:T(8,128)(2,1)S(1)}, bf16[256,2048]{1,0:T(8,128)(2,1)S(1)}, u32[]{:S(2)}, u32[]{:S(2)}) collective-permute-start(bf16[256,2048]{1,0:T(8,128)(2,1)S(1)} %get-tuple-element.16), channel_id=1, source_target_pairs={{0,32},{32,0},{1,33},{33,1},{2,34},{34,2},{3,35},{35,3},{4,36},{36... | collective-permute-start | bytes 3145736 | tf_op jit(solution)/shard_map/ppermute | solution.py:310
  142.0 4.1 %collective-permute-start.5 = (bf16[8,2048]{1,0:T(8,128)(2,1)S(1)}, bf16[8,2048]{1,0:T(8,128)(2,1)S(1)}, u32[]{:S(2)}, u32[]{:S(2)}) collective-permute-start(bf16[8,2048]{1,0:T(8,128)(2,1)S(1)} %reduce_sum.12), channel_id=1, source_target_pairs={{0,64},{64,0},{128,192},{192,128},{1,65},{65,1},{129,193},{193,129... | collective-permute-start | bytes 98312 | tf_op jit(solution)/shard_map/ppermute | solution.py:318
  146.1 10.2 %collective-permute-start.6 = (bf16[8,2048]{1,0:T(8,128)(2,1)S(1)}, bf16[8,2048]{1,0:T(8,128)(2,1)S(1)}, u32[]{:S(2)}, u32[]{:S(2)}) collective-permute-start(bf16[8,2048]{1,0:T(8,128)(2,1)S(1)} %add_convert_fusion.3), channel_id=1, source_target_pairs={{0,128},{64,192},{128,0},{192,64},{1,129},{65,193},{129,1},{193,65... | collective-permute-start | bytes 98312 | tf_op jit(solution)/shard_map/ppermute | solution.py:318
  174.7 6.5 %collective-permute-start.7 = (bf16[256,2048]{1,0:T(8,128)(2,1)S(1)}, bf16[256,2048]{1,0:T(8,128)(2,1)S(1)}, u32[]{:S(2)}, u32[]{:S(2)}) collective-permute-start(bf16[256,2048]{1,0:T(8,128)(2,1)S(1)} %bitcast.14), channel_id=1, source_target_pairs={{0,32},{32,0},{1,33},{33,1},{2,34},{34,2},{3,35},{35,3},{4,36},{36... | collective-permute-start | bytes 3145736 | tf_op jit(solution)/shard_map/ppermute | solution.py:320

commit v3 on v2

--- a/solution.py
+++ b/solution.py
@@ -34,7 +34,7 @@
 
 
 def anywhere():
-    return pl.BlockSpec(memory_space=pl.ANY)
+    return pl.BlockSpec(memory_space=pltpu.HBM)
 
 
 def dot(a, b, dims=(((1,), (0,)), ((), ()))):
@@ -141,9 +141,12 @@
             first = first + groups * step
         return carry
 
-    leaving = []
-    for i in range(query_blocks):
-        span = slice(i * QUERIES, (i + 1) * QUERIES)
+    def query_block(i, _):
+        span = pl.ds(pl.multiple_of(i * QUERIES, QUERIES), QUERIES)
+        first, last = firsts[0], lasts[0]
+        for n in range(1, query_blocks):
+            first = jnp.where(i == n, firsts[n], first)
+            last = jnp.where(i == n, lasts[n], last)
         qd = qd_ref[span, :]
         position = first_query + i * QUERIES + query_rows
         same = jnp.logical_and(position >= starts, position < ends)
@@ -161,7 +164,7 @@
             scores[j] = s
             return jnp.maximum(top, jnp.max(s.reshape(TOK // 8, 8, QUERIES), axis=0))
 
-        top = sweep(firsts[i], lasts[i], first_pass, jnp.full((8, QUERIES), -1e30, F32))
+        top = sweep(first, last, first_pass, jnp.full((8, QUERIES), -1e30, F32))
         top = jnp.max(top, axis=0, keepdims=True)
 
         def second_pass(j, carry):
@@ -174,7 +177,7 @@
             return total, attended
 
         total, attended = sweep(
-            firsts[i], lasts[i], second_pass, (jnp.zeros((8, QUERIES), F32), jnp.zeros((HEAD, QUERIES), F32))
+            first, last, second_pass, (jnp.zeros((8, QUERIES), F32), jnp.zeros((HEAD, QUERIES), F32))
         )
         share = 1.0 / jnp.sum(total, axis=0, keepdims=True)
         attended = (attended * share).astype(BF16).astype(F32)
@@ -188,16 +191,18 @@
             totals[j] += dot(both, pair)
             return grad_query + dot(turned[j, :HEAD, :], grad_scores)
 
-        grad_query = sweep(firsts[i], lasts[i], third_pass, jnp.zeros((HEAD, QUERIES), F32))
+        grad_query = sweep(first, last, third_pass, jnp.zeros((HEAD, QUERIES), F32))
         out = jnp.concatenate([attended, grad_query * HEAD**-0.5], axis=0)
         aq_ref[span, :] = out.T.astype(BF16)
-        leaving.append(pltpu.make_async_copy(aq_ref.at[span], aq_hbm.at[span], left.at[i]))
-        leaving[-1].start()
-
+        return 0
+
+    lax.fori_loop(0, query_blocks, query_block, 0)
+    leaving = [pltpu.make_async_copy(aq_ref, aq_hbm, left.at[3])]
+    leaving[0].start()
     for part, out_hbm in enumerate((kv_prev_hbm, kv_own_hbm, kv_next_hbm)):
         for j in range(per_quarter):
             kv_ref[part, j] = totals[part * per_quarter + j].astype(BF16)
-        leaving.append(pltpu.make_async_copy(kv_ref.at[part], out_hbm, left.at[query_blocks + part]))
+        leaving.append(pltpu.make_async_copy(kv_ref.at[part], out_hbm, left.at[part]))
         leaving[-1].start()
     for copy in leaving:
         copy.wait()
@@ -215,7 +220,7 @@
         scratch_shapes=[pltpu.VMEM(own.shape, BF16)] * 5 + [
             pltpu.VMEM((3, quarter // TOK, TOK, 2 * HEAD), BF16),
             pltpu.SemaphoreType.DMA((4,)),
-            pltpu.SemaphoreType.DMA((quarter // QUERIES + 3,)),
+            pltpu.SemaphoreType.DMA((4,)),
             pltpu.VMEM((blocks, TOK, 2 * HEAD), BF16),
             pltpu.VMEM((blocks, TOK, 2 * HEAD), BF16),
             pltpu.VMEM((blocks, 2 * HEAD, TOK), BF16),

time: 188 us -> 175 us (0.931)
  Pallas kernels: 32.2 us -> 22.9 us
  blocking collectives: 45.8 us -> 42.4 us
    ppermute x1, starting transfers between devices: 0.01 us -> 10.8 us  [local(): came = lax.ppermute(send, 'c', swap)]
    pallas_call x1, Pallas kernels: 28.6 us -> 19.4 us  [attention(): pl.pallas_call(attention_kernel, out_shape=(jax.ShapeDtypeStruct(own.shap...]
    ppermute x2, starting transfers between devices: 9.01 us -> 3.59 us  [local(): lax.ppermute(part, 'zh', partner).astype(F32)]
    ppermute x4, starting transfers between devices: 17.5 us -> 12.3 us  [shift(): lax.ppermute(x, 'x', [(i, i + by) for i in range(count) if 0 <= i + by <...]
    all_to_all x1, blocking collectives: 27.7 us -> 24.4 us  [local(): lax.all_to_all(part, seq_axes, 0, 0, tiled=True).astype(F32)]
    ppermute x2, waiting for transfers between devices: 5.31 us -> 7.27 us  [local(): lax.ppermute(part, 'zh', partner).astype(F32)]
where the time goes in v3:
time: 175 us; the launch traced here: 173 us
  starting transfers between devices  52.9 us (30%)
  blocking collectives  42.4 us (24%)
  waiting for transfers between devices  38.8 us (22%)
  Pallas kernels  22.9 us (13%)
  local copies, waits for them, and re-layouts  11.2 us (6%)
  other arithmetic  4.34 us (2%)
    all_to_all x1, blocking collectives, local(): lax.all_to_all(part, seq_axes, 0, 0, tiled=True).astype(F32)  24.4 us
    all_to_all x4, starting transfers between devices, exchange(): return lax.all_to_all(x, heads_axes, 0, 0, tiled=True)  21.8 us
    pallas_call x1, Pallas kernels, attention(): pl.pallas_call(attention_kernel, out_shape=(jax.ShapeDtypeStruct(own.shap...  19.4 us
    all_to_all x1, blocking collectives, spread(): lax.all_to_all(jnp.broadcast_to(x[None], (count,) + x.shape), axes, 0, 0,...  18 us
    ppermute x4, waiting for transfers between devices, shift(): lax.ppermute(x, 'x', [(i, i + by) for i in range(count) if 0 <= i + by <...  13.7 us
    all_to_all x4, waiting for transfers between devices, exchange(): return lax.all_to_all(x, heads_axes, 0, 0, tiled=True)  13.3 us
    ppermute x4, starting transfers between devices, shift(): lax.ppermute(x, 'x', [(i, i + by) for i in range(count) if 0 <= i + by <...  12.3 us
    ppermute x1, starting transfers between devices, local(): came = lax.ppermute(send, 'c', swap)  10.8 us
  transfers between devices with their start and end apart: 12, of which 11 were waited for; matrix products, arithmetic and copies ran while one was open for 1% of the time, Pallas kernels for 1%

profile of v3, /device:TPU:1, one launch (start us, length us, event | category | flops | bytes accessed | tf_op | source)
XLA Modules:
  0.0 173.3 jit_solution(17241282196602072926)
XLA Ops:
  2.5 1.0 pack.2
  3.5 6.4 %all-to-all-start = ((bf16[8,256,128]{2,1,0:T(8,128)(2,1)}), bf16[8,256,128]{2,1,0:T(8,128)(2,1)S(1)}, u32[]{:S(2)}, u32[]{:S(2)}) async-start(bf16[8,256,128]{2,1,0:T(8,128)(2,1)} %pack.2), calls=%async_computation | async-start | bytes 1048576 | tf_op jit(solution)/shard_map/all_to_all | solution.py:302
  10.9 1.0 copy-done.3
  12.8 1.2 pack.3
  14.1 3.7 %all-to-all-done = bf16[8,256,128]{2,1,0:T(8,128)(2,1)S(1)} async-done(((bf16[8,256,128]{2,1,0:T(8,128)(2,1)}), bf16[8,256,128]{2,1,0:T(8,128)(2,1)S(1)}, u32[]{:S(2)}, u32[]{:S(2)}) %all-to-all-start) | async-done | bytes 524320 | tf_op jit(solution)/shard_map/all_to_all | solution.py:302
  17.7 5.2 %all-to-all-start.1 = ((bf16[8,256,128]{2,1,0:T(8,128)(2,1)}), bf16[8,256,128]{2,1,0:T(8,128)(2,1)S(1)}, u32[]{:S(2)}, u32[]{:S(2)}) async-start(bf16[8,256,128]{2,1,0:T(8,128)(2,1)} %pack.3), calls=%async_computation.1 | async-start | bytes 1048576 | tf_op jit(solution)/shard_map/all_to_all | solution.py:302
  22.9 1.3 collective-permute-start.1
  24.2 4.0 %collective-permute-start = (bf16[2048,128]{1,0:T(8,128)(2,1)S(1)}, bf16[2048,128]{1,0:T(8,128)(2,1)S(1)}, u32[]{:S(2)}, u32[]{:S(2)}) collective-permute-start(bf16[2048,128]{1,0:T(8,128)(2,1)S(1)} %bitcast.11), channel_id=1, source_target_pairs={{0,8},{8,16},{16,24},{1,9},{9,17},{17,25},{2,10},{10,18},{18,26},{... | collective-permute-start | bytes 1572872 | tf_op jit(solution)/shard_map/ppermute | solution.py:291
  28.2 2.5 %all-to-all-done.1 = bf16[8,256,128]{2,1,0:T(8,128)(2,1)S(1)} async-done(((bf16[8,256,128]{2,1,0:T(8,128)(2,1)}), bf16[8,256,128]{2,1,0:T(8,128)(2,1)S(1)}, u32[]{:S(2)}, u32[]{:S(2)}) %all-to-all-start.1) | async-done | bytes 524320 | tf_op jit(solution)/shard_map/all_to_all | solution.py:302
  30.7 6.4 %collective-permute-done.1.next_hbm = bf16[2048,128]{1,0:T(8,128)(2,1)S(1)} collective-permute-done((bf16[2048,128]{1,0:T(8,128)(2,1)S(1)}, bf16[2048,128]{1,0:T(8,128)(2,1)S(1)}, u32[]{:S(2)}, u32[]{:S(2)}) %collective-permute-start.1) | collective-permute-done | bytes 524320 | tf_op jit(solution)/shard_map/ppermute | solution.py:291
  38.9 1.0 copy-done.6
  39.9 19.4 %attention.1 = (bf16[2048,128]{1,0:T(8,128)(2,1)}, bf16[8,256,128]{2,1,0:T(8,128)(2,1)S(1)}, bf16[8,256,128]{2,1,0:T(8,128)(2,1)S(1)}, bf16[8,256,128]{2,1,0:T(8,128)(2,1)S(1)}) custom-call(s32[1,32]{1,0:T(1,128)S(1)} %copy-done.11, s32[1]{0:T(128)} %bitcast.1.place_ref, bf16[2048,128]{1,0:T(8,128)(2,1)S(1)} %bitcast.12, bf16[2048,128]{1,0:T(8,128)(2,1)S(1)} %copy-done.6, ...), custom_call_target="tpu_custom_call" | custom-call | tf_op jit(solution)/shard_map/attention/pallas_call | solution.py:215
  61.7 5.1 %all-to-all-start.2 = ((bf16[8,256,128]{2,1,0:T(8,128)(2,1)}), bf16[8,256,128]{2,1,0:T(8,128)(2,1)S(1)}, u32[]{:S(2)}, u32[]{:S(2)}) async-start(bf16[8,256,128]{2,1,0:T(8,128)(2,1)} %bitcast.4), calls=%async_computation.2 | async-start | bytes 1048576 | tf_op jit(solution)/shard_map/all_to_all | solution.py:302
  66.8 1.3 collective-permute-start.2
  68.1 5.7 %collective-permute-start.3 = (bf16[8,256,128]{2,1,0:T(8,128)(2,1)}, bf16[8,256,128]{2,1,0:T(8,128)(2,1)S(1)}, u32[]{:S(2)}, u32[]{:S(2)}) collective-permute-start(bf16[8,256,128]{2,1,0:T(8,128)(2,1)} %copy-done.12), channel_id=1, source_target_pairs={{0,8},{8,16},{16,24},{1,9},{9,17},{17,25},{2,10},{10,18},{18,26},{... | collective-permute-start | bytes 1572872 | tf_op jit(solution)/shard_map/ppermute | solution.py:291
  73.8 5.1 %collective-permute-done.2 = bf16[8,256,128]{2,1,0:T(8,128)(2,1)S(1)} collective-permute-done((bf16[8,256,128]{2,1,0:T(8,128)(2,1)}, bf16[8,256,128]{2,1,0:T(8,128)(2,1)S(1)}, u32[]{:S(2)}, u32[]{:S(2)}) %collective-permute-start.2) | collective-permute-done | bytes 524320 | tf_op jit(solution)/shard_map/ppermute | solution.py:291
  78.9 1.3 collective-permute-done.3
  80.2 2.0 %add_convert_fusion.1 = bf16[8,256,128]{2,1,0:T(8,128)(2,1)} fusion(bf16[8,256,128]{2,1,0:T(8,128)(2,1)S(1)} %collective-permute-done.3, bf16[8,256,128]{2,1,0:T(8,128)(2,1)S(1)} %collective-permute-done.2, bf16[8,256,128]{2,1,0:T(8,128)(2,1)} %copy-done.4), kind=kLoop, calls=%fused_computation.3 | loop fusion | flops 1572864 | bytes 2097152 | tf_op jit(solution)/shard_map/convert_element_type | solution.py:310
  82.2 5.1 %all-to-all-start.3 = ((bf16[8,256,128]{2,1,0:T(8,128)(2,1)}), bf16[8,256,128]{2,1,0:T(8,128)(2,1)S(1)}, u32[]{:S(2)}, u32[]{:S(2)}) async-start(bf16[8,256,128]{2,1,0:T(8,128)(2,1)} %add_convert_fusion.1), calls=%async_computation.3 | async-start | bytes 1048576 | tf_op jit(solution)/shard_map/all_to_all | solution.py:302
  87.4 7.1 %all-to-all-done.3.kv_ref = bf16[8,256,128]{2,1,0:T(8,128)(2,1)S(1)} async-done(((bf16[8,256,128]{2,1,0:T(8,128)(2,1)}), bf16[8,256,128]{2,1,0:T(8,128)(2,1)S(1)}, u32[]{:S(2)}, u32[]{:S(2)}) %all-to-all-start.3) | async-done | bytes 524320 | tf_op jit(solution)/shard_map/all_to_all | solution.py:302
  94.5 1.3 finish.1
  95.8 10.8 %collective-permute-start.4 = (bf16[256,2048]{1,0:T(8,128)(2,1)S(1)}, bf16[256,2048]{1,0:T(8,128)(2,1)S(1)}, u32[]{:S(2)}, u32[]{:S(2)}) collective-permute-start(bf16[256,2048]{1,0:T(8,128)(2,1)S(1)} %get-tuple-element.16), channel_id=1, source_target_pairs={{0,32},{32,0},{1,33},{33,1},{2,34},{34,2},{3,35},{35,3},{4,36},{36... | collective-permute-start | bytes 3145736 | tf_op jit(solution)/shard_map/ppermute | solution.py:315
  106.6 2.3 %collective-permute-done.4 = bf16[256,2048]{1,0:T(8,128)(2,1)S(1)} collective-permute-done((bf16[256,2048]{1,0:T(8,128)(2,1)S(1)}, bf16[256,2048]{1,0:T(8,128)(2,1)S(1)}, u32[]{:S(2)}, u32[]{:S(2)}) %collective-permute-start.4) | collective-permute-done | bytes 1048608 | tf_op jit(solution)/shard_map/ppermute | solution.py:315
  109.3 24.4 %all_to_all.30 = bf16[32,8,2048]{2,1,0:T(8,128)(2,1)S(1)} all-to-all(bf16[32,8,2048]{2,1,0:T(8,128)(2,1)S(1)} %fusion), channel_id=1, replica_groups=mesh['zh'=4,'c'=2,'x'=4,'zl'=2,'y'=4] {'x','zl','y'}, dimensions={0} | all-to-all | bytes 2097152 | tf_op jit(solution)/shard_map/all_to_all | solution.py:319
  133.9 4.0 %collective-permute-done.5 = bf16[8,2048]{1,0:T(8,128)(2,1)S(1)} collective-permute-done((bf16[8,2048]{1,0:T(8,128)(2,1)S(1)}, bf16[8,2048]{1,0:T(8,128)(2,1)S(1)}, u32[]{:S(2)}, u32[]{:S(2)}) %collective-permute-start.5) | collective-permute-done | bytes 32800 | tf_op jit(solution)/shard_map/ppermute | solution.py:323
  137.9 3.5 %collective-permute-start.6 = (bf16[8,2048]{1,0:T(8,128)(2,1)S(1)}, bf16[8,2048]{1,0:T(8,128)(2,1)S(1)}, u32[]{:S(2)}, u32[]{:S(2)}) collective-permute-start(bf16[8,2048]{1,0:T(8,128)(2,1)S(1)} %add_convert_fusion.3), channel_id=1, source_target_pairs={{0,128},{64,192},{128,0},{192,64},{1,129},{65,193},{129,1},{193,65... | collective-permute-start | bytes 98312 | tf_op jit(solution)/shard_map/ppermute | solution.py:323
  141.4 3.3 %collective-permute-done.6 = bf16[8,2048]{1,0:T(8,128)(2,1)S(1)} collective-permute-done((bf16[8,2048]{1,0:T(8,128)(2,1)S(1)}, bf16[8,2048]{1,0:T(8,128)(2,1)S(1)}, u32[]{:S(2)}, u32[]{:S(2)}) %collective-permute-start.6) | collective-permute-done | bytes 32800 | tf_op jit(solution)/shard_map/ppermute | solution.py:323
  144.8 18.0 %all_to_all.31 = bf16[32,8,2048]{2,1,0:T(8,128)(2,1)S(1)} all-to-all(bf16[32,8,2048]{2,1,0:T(8,128)(2,1)S(1)} %broadcast_in_dim.2), channel_id=1, replica_groups=mesh['zh'=4,'c'=2,'x'=4,'zl'=2,'y'=4] {'x','zl','y'}, dimensions={0} | all-to-all | bytes 2097152 | tf_op jit(solution)/shard_map/all_to_all | solution.py:286
  162.8 4.5 %collective-permute-start.7 = (bf16[256,2048]{1,0:T(8,128)(2,1)S(1)}, bf16[256,2048]{1,0:T(8,128)(2,1)S(1)}, u32[]{:S(2)}, u32[]{:S(2)}) collective-permute-start(bf16[256,2048]{1,0:T(8,128)(2,1)S(1)} %bitcast.14), channel_id=1, source_target_pairs={{0,32},{32,0},{1,33},{33,1},{2,34},{34,2},{3,35},{35,3},{4,36},{36... | collective-permute-start | bytes 3145736 | tf_op jit(solution)/shard_map/ppermute | solution.py:325
  167.3 2.3 %collective-permute-done.7 = bf16[256,2048]{1,0:T(8,128)(2,1)S(1)} collective-permute-done((bf16[256,2048]{1,0:T(8,128)(2,1)S(1)}, bf16[256,2048]{1,0:T(8,128)(2,1)S(1)}, u32[]{:S(2)}, u32[]{:S(2)}) %collective-permute-start.7) | collective-permute-done | bytes 1048608 | tf_op jit(solution)/shard_map/ppermute | solution.py:325
  169.8 1.1 maximum_convert_fusion.1
  171.4 2.0 %slice.8 = f32[512,1536]{1,0:T(8,128)} slice(f32[512,2048]{1,0:T(8,128)S(1)} %maximum_convert_fusion), slice={[0:512], [0:1536]} | slice | bytes 6291456 | tf_op jit(solution)/shard_map/slice | solution.py:330
  (36 shorter events, 9.3 us)
Async XLA Ops:
  0.6 1.0 copy-start.7
  1.6 0.9 copy-start.8
  2.5 36.3 %copy-start.11 = (s32[1,32]{1,0:T(1,128)S(1)}, s32[1,32]{1,0:T(1,128)}, u32[]{:S(2)}) copy-start(s32[1,32]{1,0:T(1,128)} %tiles_ref.1) | copy-start | bytes 388
  3.5 14.2 %all-to-all-start = ((bf16[8,256,128]{2,1,0:T(8,128)(2,1)}), bf16[8,256,128]{2,1,0:T(8,128)(2,1)S(1)}, u32[]{:S(2)}, u32[]{:S(2)}) async-start(bf16[8,256,128]{2,1,0:T(8,128)(2,1)} %pack.2), calls=%async_computation | async-start | bytes 1048576 | tf_op jit(solution)/shard_map/all_to_all | solution.py:302
  9.9 0.9 copy-start.1
  10.9 1.0 copy-start.3
  11.9 0.9 copy-start.9
  17.7 13.0 %all-to-all-start.1 = ((bf16[8,256,128]{2,1,0:T(8,128)(2,1)}), bf16[8,256,128]{2,1,0:T(8,128)(2,1)S(1)}, u32[]{:S(2)}, u32[]{:S(2)}) async-start(bf16[8,256,128]{2,1,0:T(8,128)(2,1)} %pack.3), calls=%async_computation.1 | async-start | bytes 1048576 | tf_op jit(solution)/shard_map/all_to_all | solution.py:302
  22.9 14.2 %collective-permute-start.1 = (bf16[2048,128]{1,0:T(8,128)(2,1)S(1)}, bf16[2048,128]{1,0:T(8,128)(2,1)S(1)}, u32[]{:S(2)}, u32[]{:S(2)}) collective-permute-start(bf16[2048,128]{1,0:T(8,128)(2,1)S(1)} %bitcast.10), channel_id=1, source_target_pairs={{8,0},{16,8},{24,16},{9,1},{17,9},{25,17},{10,2},{18,10},{26,18},{... | collective-permute-start | bytes 1572872 | tf_op jit(solution)/shard_map/ppermute | solution.py:291
  24.2 13.9 %collective-permute-start = (bf16[2048,128]{1,0:T(8,128)(2,1)S(1)}, bf16[2048,128]{1,0:T(8,128)(2,1)S(1)}, u32[]{:S(2)}, u32[]{:S(2)}) collective-permute-start(bf16[2048,128]{1,0:T(8,128)(2,1)S(1)} %bitcast.11), channel_id=1, source_target_pairs={{0,8},{8,16},{16,24},{1,9},{9,17},{17,25},{2,10},{10,18},{18,26},{... | collective-permute-start | bytes 1572872 | tf_op jit(solution)/shard_map/ppermute | solution.py:291
  38.1 0.8 copy-start.5
  38.8 1.0 copy-start.6
  39.9 54.6 %copy-start = (bf16[512,1536]{1,0:T(8,128)(2,1)S(1)}, bf16[512,1536]{1,0:T(8,128)(2,1)}, u32[]{:S(2)}) copy-start(bf16[512,1536]{1,0:T(8,128)(2,1)} %wqkv_ref.1) | copy-start | bytes 4718596
  39.9 54.6 %copy-start.2 = (bf16[1,256,512]{2,1,0:T(8,128)(2,1)S(1)}, bf16[1,256,512]{2,1,0:T(8,128)(2,1)}, u32[]{:S(2)}) copy-start(bf16[1,256,512]{2,1,0:T(8,128)(2,1)} %gout_ref.1) | copy-start | bytes 786436
  59.3 0.8 copy-start.4
  60.1 0.8 copy-start.12
  60.9 0.8 copy-start.13
  61.7 32.8 %copy-start.10 = (bf16[1,256,512]{2,1,0:T(8,128)(2,1)S(1)}, bf16[1,256,512]{2,1,0:T(8,128)(2,1)}, u32[]{:S(2)}) copy-start(bf16[1,256,512]{2,1,0:T(8,128)(2,1)} %normed_ref.1) | copy-start | bytes 786436
  61.7 20.5 %all-to-all-start.2 = ((bf16[8,256,128]{2,1,0:T(8,128)(2,1)}), bf16[8,256,128]{2,1,0:T(8,128)(2,1)S(1)}, u32[]{:S(2)}, u32[]{:S(2)}) async-start(bf16[8,256,128]{2,1,0:T(8,128)(2,1)} %bitcast.4), calls=%async_computation.2 | async-start | bytes 1048576 | tf_op jit(solution)/shard_map/all_to_all | solution.py:302
  66.8 12.1 %collective-permute-start.2 = (bf16[8,256,128]{2,1,0:T(8,128)(2,1)}, bf16[8,256,128]{2,1,0:T(8,128)(2,1)S(1)}, u32[]{:S(2)}, u32[]{:S(2)}) collective-permute-start(bf16[8,256,128]{2,1,0:T(8,128)(2,1)} %copy-done.13), channel_id=1, source_target_pairs={{8,0},{16,8},{24,16},{9,1},{17,9},{25,17},{10,2},{18,10},{26,18},{... | collective-permute-start | bytes 1572872 | tf_op jit(solution)/shard_map/ppermute | solution.py:291
  68.1 12.1 %collective-permute-start.3 = (bf16[8,256,128]{2,1,0:T(8,128)(2,1)}, bf16[8,256,128]{2,1,0:T(8,128)(2,1)S(1)}, u32[]{:S(2)}, u32[]{:S(2)}) collective-permute-start(bf16[8,256,128]{2,1,0:T(8,128)(2,1)} %copy-done.12), channel_id=1, source_target_pairs={{0,8},{8,16},{16,24},{1,9},{9,17},{17,25},{2,10},{10,18},{18,26},{... | collective-permute-start | bytes 1572872 | tf_op jit(solution)/shard_map/ppermute | solution.py:291
  82.2 12.3 %all-to-all-start.3 = ((bf16[8,256,128]{2,1,0:T(8,128)(2,1)}), bf16[8,256,128]{2,1,0:T(8,128)(2,1)S(1)}, u32[]{:S(2)}, u32[]{:S(2)}) async-start(bf16[8,256,128]{2,1,0:T(8,128)(2,1)} %add_convert_fusion.1), calls=%async_computation.3 | async-start | bytes 1048576 | tf_op jit(solution)/shard_map/all_to_all | solution.py:302
  95.8 13.0 %collective-permute-start.4 = (bf16[256,2048]{1,0:T(8,128)(2,1)S(1)}, bf16[256,2048]{1,0:T(8,128)(2,1)S(1)}, u32[]{:S(2)}, u32[]{:S(2)}) collective-permute-start(bf16[256,2048]{1,0:T(8,128)(2,1)S(1)} %get-tuple-element.16), channel_id=1, source_target_pairs={{0,32},{32,0},{1,33},{33,1},{2,34},{34,2},{3,35},{35,3},{4,36},{36... | collective-permute-start | bytes 3145736 | tf_op jit(solution)/shard_map/ppermute | solution.py:315
  133.8 4.1 %collective-permute-start.5 = (bf16[8,2048]{1,0:T(8,128)(2,1)S(1)}, bf16[8,2048]{1,0:T(8,128)(2,1)S(1)}, u32[]{:S(2)}, u32[]{:S(2)}) collective-permute-start(bf16[8,2048]{1,0:T(8,128)(2,1)S(1)} %reduce_sum.12), channel_id=1, source_target_pairs={{0,64},{64,0},{128,192},{192,128},{1,65},{65,1},{129,193},{193,129... | collective-permute-start | bytes 98312 | tf_op jit(solution)/shard_map/ppermute | solution.py:323
  137.9 6.8 %collective-permute-start.6 = (bf16[8,2048]{1,0:T(8,128)(2,1)S(1)}, bf16[8,2048]{1,0:T(8,128)(2,1)S(1)}, u32[]{:S(2)}, u32[]{:S(2)}) collective-permute-start(bf16[8,2048]{1,0:T(8,128)(2,1)S(1)} %add_convert_fusion.3), channel_id=1, source_target_pairs={{0,128},{64,192},{128,0},{192,64},{1,129},{65,193},{129,1},{193,65... | collective-permute-start | bytes 98312 | tf_op jit(solution)/shard_map/ppermute | solution.py:323
  162.8 6.8 %collective-permute-start.7 = (bf16[256,2048]{1,0:T(8,128)(2,1)S(1)}, bf16[256,2048]{1,0:T(8,128)(2,1)S(1)}, u32[]{:S(2)}, u32[]{:S(2)}) collective-permute-start(bf16[256,2048]{1,0:T(8,128)(2,1)S(1)} %bitcast.14), channel_id=1, source_target_pairs={{0,32},{32,0},{1,33},{33,1},{2,34},{34,2},{3,35},{35,3},{4,36},{36... | collective-permute-start | bytes 3145736 | tf_op jit(solution)/shard_map/ppermute | solution.py:325

commit v4 on v3

--- a/solution.py
+++ b/solution.py
@@ -282,6 +282,35 @@
     )(*arrays)
 
 
+def place_kernel(core_ref, mine_ref, other_ref, qkv_ref, out_ref):
+    rows = mine_ref.shape[0]
+    split = qkv_ref.shape[1]
+
+    def lay(*halves):
+        for n, ref in enumerate(halves):
+            spot = slice(n * rows, (n + 1) * rows)
+            qkv_ref[spot, :] = ref[:, :split].astype(F32)
+            out_ref[spot, :] = ref[:, split:].astype(F32)
+
+    pl.when(core_ref[0] == 0)(lambda: lay(mine_ref, other_ref))
+    pl.when(core_ref[0] != 0)(lambda: lay(other_ref, mine_ref))
+
+
+def place_sums(core, mine, other):
+    width = HEADS * HEAD
+    return pl.pallas_call(
+        place_kernel,
+        out_shape=(
+            jax.ShapeDtypeStruct((width, 3 * width), F32),
+            jax.ShapeDtypeStruct((width, width), F32),
+        ),
+        in_specs=[smem()] + [vmem()] * 2,
+        out_specs=(vmem(),) * 2,
+        compiler_params=params(),
+        name="place_sums",
+    )(core, mine, other)
+
+
 def spread(x, axes, count):
     return lax.all_to_all(jnp.broadcast_to(x[None], (count,) + x.shape), axes, 0, 0, tiled=True)
 
@@ -323,11 +352,8 @@
         part = (part.astype(F32) + lax.ppermute(part, "zh", partner).astype(F32)).astype(BF16)
     mine = spread(part, seq_axes, seq_count).reshape(rows, columns)
     other = lax.ppermute(mine, "c", swap)
-    first = core[0] == 0
-    total = jnp.concatenate([jnp.where(first, mine, other), jnp.where(first, other, mine)], axis=0)
-    total = total.astype(F32)
-    joint_width = w_qkv.shape[1]
-    return grad_in, total[:, :joint_width], total[:, joint_width:]
+    total_qkv, total_out = place_sums(core, mine, other)
+    return grad_in, total_qkv, total_out
 
 
 def solution(mesh):

time: 175 us -> 171 us (0.977)
  blocking collectives: 42.4 us -> 49 us
  local copies, waits for them, and re-layouts: 11.2 us -> 4.63 us
  other arithmetic: 4.34 us -> 1.56 us
  Pallas kernels: 22.9 us -> 20.9 us
  waiting for transfers between devices: 38.8 us -> 40.7 us
    all_to_all x1, blocking collectives: 24.4 us -> 30.7 us  [local(): lax.all_to_all(part, seq_axes, 0, 0, tiled=True).astype(F32)]
    ppermute x2, starting transfers between devices: 3.59 us -> 8.46 us  [local(): lax.ppermute(part, 'zh', partner).astype(F32)]
    unnamed x28 -> x20, local copies, waits for them, and re-layouts: 9.09 us -> 4.52 us
    pallas_call x1, Pallas kernels: 19.4 us -> 15 us  [attention(): pl.pallas_call(attention_kernel, out_shape=(jax.ShapeDtypeStruct(own.shap...]
    ppermute x1, starting transfers between devices: 10.8 us -> 7.21 us  [local(): came = lax.ppermute(send, 'c', swap)]
    all_to_all x4, waiting for transfers between devices: 13.3 us -> 16.2 us  [exchange(): return lax.all_to_all(x, heads_axes, 0, 0, tiled=True)]
    pallas_call x0 -> x1, Pallas kernels: none -> 2.28 us  [place_sums(): pl.pallas_call(place_kernel, out_shape=(jax.ShapeDtypeStruct((width, 3 *...]
    slice x1 -> x0, local copies, waits for them, and re-layouts: 1.96 us -> none  [local(): return (grad_in, total[:, :joint_width], total[:, joint_width:])]
where the time goes in v4:
time: 171 us; the launch traced here: 170 us
  starting transfers between devices  52.9 us (31%)
  blocking collectives  49 us (29%)
  waiting for transfers between devices  40.7 us (24%)
  Pallas kernels  20.9 us (12%)
  local copies, waits for them, and re-layouts  4.63 us (3%)
    all_to_all x1, blocking collectives, local(): lax.all_to_all(part, seq_axes, 0, 0, tiled=True).astype(F32)  30.7 us
    all_to_all x4, starting transfers between devices, exchange(): return lax.all_to_all(x, heads_axes, 0, 0, tiled=True)  21.6 us
    all_to_all x1, blocking collectives, spread(): lax.all_to_all(jnp.broadcast_to(x[None], (count,) + x.shape), axes, 0, 0,...  18.3 us
    all_to_all x4, waiting for transfers between devices, exchange(): return lax.all_to_all(x, heads_axes, 0, 0, tiled=True)  16.2 us
    pallas_call x1, Pallas kernels, attention(): pl.pallas_call(attention_kernel, out_shape=(jax.ShapeDtypeStruct(own.shap...  15 us
    ppermute x4, waiting for transfers between devices, shift(): lax.ppermute(x, 'x', [(i, i + by) for i in range(count) if 0 <= i + by <...  14.4 us
    ppermute x4, starting transfers between devices, shift(): lax.ppermute(x, 'x', [(i, i + by) for i in range(count) if 0 <= i + by <...  11.9 us
    ppermute x2, starting transfers between devices, local(): lax.ppermute(part, 'zh', partner).astype(F32)  8.46 us
  transfers between devices with their start and end apart: 12, of which 11 were waited for; matrix products, arithmetic and copies ran while one was open for 1% of the time, Pallas kernels for 1%

profile of v4, /device:TPU:1, one launch (start us, length us, event | category | flops | bytes accessed | tf_op | source)
XLA Modules:
  0.0 170.4 jit_solution(5715653121787068933)
XLA Ops:
  0.7 1.0 copy-done.3
  1.7 0.9 copy-done.4
  2.6 1.0 pack.2
  3.6 6.5 %all-to-all-start = ((bf16[8,256,128]{2,1,0:T(8,128)(2,1)}), bf16[8,256,128]{2,1,0:T(8,128)(2,1)S(1)}, u32[]{:S(2)}, u32[]{:S(2)}) async-start(bf16[8,256,128]{2,1,0:T(8,128)(2,1)} %pack.2), calls=%async_computation | async-start | bytes 1048576 | tf_op jit(solution)/shard_map/all_to_all | solution.py:331
  10.2 1.2 pack.3
  11.4 6.6 %all-to-all-done = bf16[8,256,128]{2,1,0:T(8,128)(2,1)S(1)} async-done(((bf16[8,256,128]{2,1,0:T(8,128)(2,1)}), bf16[8,256,128]{2,1,0:T(8,128)(2,1)S(1)}, u32[]{:S(2)}, u32[]{:S(2)}) %all-to-all-start) | async-done | bytes 524320 | tf_op jit(solution)/shard_map/all_to_all | solution.py:331
  17.9 5.2 %all-to-all-start.1 = ((bf16[8,256,128]{2,1,0:T(8,128)(2,1)}), bf16[8,256,128]{2,1,0:T(8,128)(2,1)S(1)}, u32[]{:S(2)}, u32[]{:S(2)}) async-start(bf16[8,256,128]{2,1,0:T(8,128)(2,1)} %pack.3), calls=%async_computation.1 | async-start | bytes 1048576 | tf_op jit(solution)/shard_map/all_to_all | solution.py:331
  23.1 1.3 collective-permute-start.1
  24.4 4.0 %collective-permute-start = (bf16[2048,128]{1,0:T(8,128)(2,1)S(1)}, bf16[2048,128]{1,0:T(8,128)(2,1)S(1)}, u32[]{:S(2)}, u32[]{:S(2)}) collective-permute-start(bf16[2048,128]{1,0:T(8,128)(2,1)S(1)} %bitcast.11), channel_id=1, source_target_pairs={{0,8},{8,16},{16,24},{1,9},{9,17},{17,25},{2,10},{10,18},{18,26},{... | collective-permute-start | bytes 1572872 | tf_op jit(solution)/shard_map/ppermute | solution.py:320
  28.4 2.5 %all-to-all-done.1 = bf16[8,256,128]{2,1,0:T(8,128)(2,1)S(1)} async-done(((bf16[8,256,128]{2,1,0:T(8,128)(2,1)}), bf16[8,256,128]{2,1,0:T(8,128)(2,1)S(1)}, u32[]{:S(2)}, u32[]{:S(2)}) %all-to-all-start.1) | async-done | bytes 524320 | tf_op jit(solution)/shard_map/all_to_all | solution.py:331
  30.9 6.4 %collective-permute-done.1.next_hbm = bf16[2048,128]{1,0:T(8,128)(2,1)S(1)} collective-permute-done((bf16[2048,128]{1,0:T(8,128)(2,1)S(1)}, bf16[2048,128]{1,0:T(8,128)(2,1)S(1)}, u32[]{:S(2)}, u32[]{:S(2)}) %collective-permute-start.1) | collective-permute-done | bytes 524320 | tf_op jit(solution)/shard_map/ppermute | solution.py:320
  38.3 15.0 %attention.1 = (bf16[2048,128]{1,0:T(8,128)(2,1)}, bf16[8,256,128]{2,1,0:T(8,128)(2,1)S(1)}, bf16[8,256,128]{2,1,0:T(8,128)(2,1)S(1)}, bf16[8,256,128]{2,1,0:T(8,128)(2,1)S(1)}) custom-call(s32[1,32]{1,0:T(1,128)S(1)} %copy-done.7, s32[1]{0:T(128)} %bitcast.1.place_ref, bf16[2048,128]{1,0:T(8,128)(2,1)S(1)} %bitcast.12, ...), custom_call_target="tpu_custom_call" | custom-call | tf_op jit(solution)/shard_map/attention/pallas_call | solution.py:215
  54.9 5.1 %all-to-all-start.2 = ((bf16[8,256,128]{2,1,0:T(8,128)(2,1)}), bf16[8,256,128]{2,1,0:T(8,128)(2,1)S(1)}, u32[]{:S(2)}, u32[]{:S(2)}) async-start(bf16[8,256,128]{2,1,0:T(8,128)(2,1)} %bitcast.4), calls=%async_computation.2 | async-start | bytes 1048576 | tf_op jit(solution)/shard_map/all_to_all | solution.py:331
  60.0 1.3 collective-permute-start.2
  61.3 5.3 %collective-permute-start.3 = (bf16[8,256,128]{2,1,0:T(8,128)(2,1)}, bf16[8,256,128]{2,1,0:T(8,128)(2,1)S(1)}, u32[]{:S(2)}, u32[]{:S(2)}) collective-permute-start(bf16[8,256,128]{2,1,0:T(8,128)(2,1)} %copy-done.8), channel_id=1, source_target_pairs={{0,8},{8,16},{16,24},{1,9},{9,17},{17,25},{2,10},{10,18},{18,26},{... | collective-permute-start | bytes 1572872 | tf_op jit(solution)/shard_map/ppermute | solution.py:320
  66.6 6.0 %collective-permute-done.2 = bf16[8,256,128]{2,1,0:T(8,128)(2,1)S(1)} collective-permute-done((bf16[8,256,128]{2,1,0:T(8,128)(2,1)}, bf16[8,256,128]{2,1,0:T(8,128)(2,1)S(1)}, u32[]{:S(2)}, u32[]{:S(2)}) %collective-permute-start.2) | collective-permute-done | bytes 524320 | tf_op jit(solution)/shard_map/ppermute | solution.py:320
  72.6 1.0 collective-permute-done.3
  73.6 1.0 add_convert_fusion.1
  74.6 4.9 %all-to-all-start.3 = ((bf16[8,256,128]{2,1,0:T(8,128)(2,1)}), bf16[8,256,128]{2,1,0:T(8,128)(2,1)S(1)}, u32[]{:S(2)}, u32[]{:S(2)}) async-start(bf16[8,256,128]{2,1,0:T(8,128)(2,1)} %add_convert_fusion.1), calls=%async_computation.3 | async-start | bytes 1048576 | tf_op jit(solution)/shard_map/all_to_all | solution.py:331
  79.5 7.1 %all-to-all-done.3.kv_ref = bf16[8,256,128]{2,1,0:T(8,128)(2,1)S(1)} async-done(((bf16[8,256,128]{2,1,0:T(8,128)(2,1)}), bf16[8,256,128]{2,1,0:T(8,128)(2,1)S(1)}, u32[]{:S(2)}, u32[]{:S(2)}) %all-to-all-start.3) | async-done | bytes 524320 | tf_op jit(solution)/shard_map/all_to_all | solution.py:331
  86.6 0.9 copy-done.6
  87.6 1.3 finish.1
  88.9 7.2 %collective-permute-start.4 = (bf16[256,2048]{1,0:T(8,128)(2,1)S(1)}, bf16[256,2048]{1,0:T(8,128)(2,1)S(1)}, u32[]{:S(2)}, u32[]{:S(2)}) collective-permute-start(bf16[256,2048]{1,0:T(8,128)(2,1)S(1)} %get-tuple-element.18), channel_id=1, source_target_pairs={{0,32},{32,0},{1,33},{33,1},{2,34},{34,2},{3,35},{35,3},{4,36},{36... | collective-permute-start | bytes 3145736 | tf_op jit(solution)/shard_map/ppermute | solution.py:344
  96.1 2.3 %collective-permute-done.4 = bf16[256,2048]{1,0:T(8,128)(2,1)S(1)} collective-permute-done((bf16[256,2048]{1,0:T(8,128)(2,1)S(1)}, bf16[256,2048]{1,0:T(8,128)(2,1)S(1)}, u32[]{:S(2)}, u32[]{:S(2)}) %collective-permute-start.4) | collective-permute-done | bytes 1048608 | tf_op jit(solution)/shard_map/ppermute | solution.py:344
  98.8 30.7 %all_to_all.30 = bf16[32,8,2048]{2,1,0:T(8,128)(2,1)S(1)} all-to-all(bf16[32,8,2048]{2,1,0:T(8,128)(2,1)S(1)} %fusion), channel_id=1, replica_groups=mesh['zh'=4,'c'=2,'x'=4,'zl'=2,'y'=4] {'x','zl','y'}, dimensions={0} | all-to-all | bytes 2097152 | tf_op jit(solution)/shard_map/all_to_all | solution.py:348
  129.8 4.0 %collective-permute-done.5 = bf16[8,2048]{1,0:T(8,128)(2,1)S(1)} collective-permute-done((bf16[8,2048]{1,0:T(8,128)(2,1)S(1)}, bf16[8,2048]{1,0:T(8,128)(2,1)S(1)}, u32[]{:S(2)}, u32[]{:S(2)}) %collective-permute-start.5) | collective-permute-done | bytes 32800 | tf_op jit(solution)/shard_map/ppermute | solution.py:352
  133.8 8.4 %collective-permute-start.6 = (bf16[8,2048]{1,0:T(8,128)(2,1)S(1)}, bf16[8,2048]{1,0:T(8,128)(2,1)S(1)}, u32[]{:S(2)}, u32[]{:S(2)}) collective-permute-start(bf16[8,2048]{1,0:T(8,128)(2,1)S(1)} %add_convert_fusion.3), channel_id=1, source_target_pairs={{0,128},{64,192},{128,0},{192,64},{1,129},{65,193},{129,1},{193,65... | collective-permute-start | bytes 98312 | tf_op jit(solution)/shard_map/ppermute | solution.py:352
  142.2 1.6 collective-permute-done.6
  143.9 18.3 %all_to_all.31 = bf16[32,8,2048]{2,1,0:T(8,128)(2,1)S(1)} all-to-all(bf16[32,8,2048]{2,1,0:T(8,128)(2,1)S(1)} %broadcast_in_dim.2), channel_id=1, replica_groups=mesh['zh'=4,'c'=2,'x'=4,'zl'=2,'y'=4] {'x','zl','y'}, dimensions={0} | all-to-all | bytes 2097152 | tf_op jit(solution)/shard_map/all_to_all | solution.py:315
  162.2 3.7 %collective-permute-start.7 = (bf16[256,2048]{1,0:T(8,128)(2,1)S(1)}, bf16[256,2048]{1,0:T(8,128)(2,1)S(1)}, u32[]{:S(2)}, u32[]{:S(2)}) collective-permute-start(bf16[256,2048]{1,0:T(8,128)(2,1)S(1)} %bitcast.8), channel_id=1, source_target_pairs={{0,32},{32,0},{1,33},{33,1},{2,34},{34,2},{3,35},{35,3},{4,36},{36... | collective-permute-start | bytes 3145736 | tf_op jit(solution)/shard_map/ppermute | solution.py:354
  165.9 2.3 %collective-permute-done.7.other_ref = bf16[256,2048]{1,0:T(8,128)(2,1)S(1)} collective-permute-done((bf16[256,2048]{1,0:T(8,128)(2,1)S(1)}, bf16[256,2048]{1,0:T(8,128)(2,1)S(1)}, u32[]{:S(2)}, u32[]{:S(2)}) %collective-permute-start.7) | collective-permute-done | bytes 1048608 | tf_op jit(solution)/shard_map/ppermute | solution.py:354
  168.2 2.3 %place_sums.1 = (f32[512,1536]{1,0:T(8,128)}, f32[512,512]{1,0:T(8,128)}) custom-call(s32[1]{0:T(128)} %bitcast.core_ref, bf16[256,2048]{1,0:T(8,128)(2,1)S(1)} %bitcast.9, bf16[256,2048]{1,0:T(8,128)(2,1)S(1)} %collective-permute-done.7.other_ref), custom_call_target="tpu_custom_call" | custom-call | tf_op jit(solution)/shard_map/place_sums/pallas_call | solution.py:301
  (25 shorter events, 3.3 us)
Async XLA Ops:
  0.6 9.5 %copy-start.1 = (bf16[1,256,512]{2,1,0:T(8,128)(2,1)S(1)}, bf16[1,256,512]{2,1,0:T(8,128)(2,1)}, u32[]{:S(2)}) copy-start(bf16[1,256,512]{2,1,0:T(8,128)(2,1)} %gout_ref.1) | copy-start | bytes 786436
  0.6 9.5 %copy-start.2 = (bf16[512,512]{1,0:T(8,128)(2,1)S(1)}, bf16[512,512]{1,0:T(8,128)(2,1)}, u32[]{:S(2)}) copy-start(bf16[512,512]{1,0:T(8,128)(2,1)} %w_ref.1) | copy-start | bytes 1572868
  0.7 1.0 copy-start.3
  1.7 0.9 copy-start.4
  2.6 7.5 %copy-start.5 = (bf16[1,256,512]{2,1,0:T(8,128)(2,1)S(1)}, bf16[1,256,512]{2,1,0:T(8,128)(2,1)}, u32[]{:S(2)}) copy-start(bf16[1,256,512]{2,1,0:T(8,128)(2,1)} %q_ref.1) | copy-start | bytes 786436
  3.6 34.7 %copy-start.7 = (s32[1,32]{1,0:T(1,128)S(1)}, s32[1,32]{1,0:T(1,128)}, u32[]{:S(2)}) copy-start(s32[1,32]{1,0:T(1,128)} %tiles_ref.1) | copy-start | bytes 388
  3.6 14.3 %all-to-all-start = ((bf16[8,256,128]{2,1,0:T(8,128)(2,1)}), bf16[8,256,128]{2,1,0:T(8,128)(2,1)S(1)}, u32[]{:S(2)}, u32[]{:S(2)}) async-start(bf16[8,256,128]{2,1,0:T(8,128)(2,1)} %pack.2), calls=%async_computation | async-start | bytes 1048576 | tf_op jit(solution)/shard_map/all_to_all | solution.py:331
  17.9 13.0 %all-to-all-start.1 = ((bf16[8,256,128]{2,1,0:T(8,128)(2,1)}), bf16[8,256,128]{2,1,0:T(8,128)(2,1)S(1)}, u32[]{:S(2)}, u32[]{:S(2)}) async-start(bf16[8,256,128]{2,1,0:T(8,128)(2,1)} %pack.3), calls=%async_computation.1 | async-start | bytes 1048576 | tf_op jit(solution)/shard_map/all_to_all | solution.py:331
  23.1 14.2 %collective-permute-start.1 = (bf16[2048,128]{1,0:T(8,128)(2,1)S(1)}, bf16[2048,128]{1,0:T(8,128)(2,1)S(1)}, u32[]{:S(2)}, u32[]{:S(2)}) collective-permute-start(bf16[2048,128]{1,0:T(8,128)(2,1)S(1)} %bitcast.10), channel_id=1, source_target_pairs={{8,0},{16,8},{24,16},{9,1},{17,9},{25,17},{10,2},{18,10},{26,18},{... | collective-permute-start | bytes 1572872 | tf_op jit(solution)/shard_map/ppermute | solution.py:320
  24.4 13.9 %collective-permute-start = (bf16[2048,128]{1,0:T(8,128)(2,1)S(1)}, bf16[2048,128]{1,0:T(8,128)(2,1)S(1)}, u32[]{:S(2)}, u32[]{:S(2)}) collective-permute-start(bf16[2048,128]{1,0:T(8,128)(2,1)S(1)} %bitcast.11), channel_id=1, source_target_pairs={{0,8},{8,16},{16,24},{1,9},{9,17},{17,25},{2,10},{10,18},{18,26},{... | collective-permute-start | bytes 1572872 | tf_op jit(solution)/shard_map/ppermute | solution.py:320
  53.3 0.8 copy-start.8
  54.1 0.8 copy-start.9
  54.9 31.7 %copy-start = (bf16[512,1536]{1,0:T(8,128)(2,1)S(1)}, bf16[512,1536]{1,0:T(8,128)(2,1)}, u32[]{:S(2)}) copy-start(bf16[512,1536]{1,0:T(8,128)(2,1)} %wqkv_ref.1) | copy-start | bytes 4718596
  54.9 19.7 %all-to-all-start.2 = ((bf16[8,256,128]{2,1,0:T(8,128)(2,1)}), bf16[8,256,128]{2,1,0:T(8,128)(2,1)S(1)}, u32[]{:S(2)}, u32[]{:S(2)}) async-start(bf16[8,256,128]{2,1,0:T(8,128)(2,1)} %bitcast.4), calls=%async_computation.2 | async-start | bytes 1048576 | tf_op jit(solution)/shard_map/all_to_all | solution.py:331
  60.0 12.6 %collective-permute-start.2 = (bf16[8,256,128]{2,1,0:T(8,128)(2,1)}, bf16[8,256,128]{2,1,0:T(8,128)(2,1)S(1)}, u32[]{:S(2)}, u32[]{:S(2)}) collective-permute-start(bf16[8,256,128]{2,1,0:T(8,128)(2,1)} %copy-done.9), channel_id=1, source_target_pairs={{8,0},{16,8},{24,16},{9,1},{17,9},{25,17},{10,2},{18,10},{26,18},{... | collective-permute-start | bytes 1572872 | tf_op jit(solution)/shard_map/ppermute | solution.py:320
  61.3 12.3 %collective-permute-start.3 = (bf16[8,256,128]{2,1,0:T(8,128)(2,1)}, bf16[8,256,128]{2,1,0:T(8,128)(2,1)S(1)}, u32[]{:S(2)}, u32[]{:S(2)}) collective-permute-start(bf16[8,256,128]{2,1,0:T(8,128)(2,1)} %copy-done.8), channel_id=1, source_target_pairs={{0,8},{8,16},{16,24},{1,9},{9,17},{17,25},{2,10},{10,18},{18,26},{... | collective-permute-start | bytes 1572872 | tf_op jit(solution)/shard_map/ppermute | solution.py:320
  74.6 12.0 %all-to-all-start.3 = ((bf16[8,256,128]{2,1,0:T(8,128)(2,1)}), bf16[8,256,128]{2,1,0:T(8,128)(2,1)S(1)}, u32[]{:S(2)}, u32[]{:S(2)}) async-start(bf16[8,256,128]{2,1,0:T(8,128)(2,1)} %add_convert_fusion.1), calls=%async_computation.3 | async-start | bytes 1048576 | tf_op jit(solution)/shard_map/all_to_all | solution.py:331
  86.6 1.0 copy-start.6
  88.9 9.5 %collective-permute-start.4 = (bf16[256,2048]{1,0:T(8,128)(2,1)S(1)}, bf16[256,2048]{1,0:T(8,128)(2,1)S(1)}, u32[]{:S(2)}, u32[]{:S(2)}) collective-permute-start(bf16[256,2048]{1,0:T(8,128)(2,1)S(1)} %get-tuple-element.18), channel_id=1, source_target_pairs={{0,32},{32,0},{1,33},{33,1},{2,34},{34,2},{3,35},{35,3},{4,36},{36... | collective-permute-start | bytes 3145736 | tf_op jit(solution)/shard_map/ppermute | solution.py:344
  129.7 4.1 %collective-permute-start.5 = (bf16[8,2048]{1,0:T(8,128)(2,1)S(1)}, bf16[8,2048]{1,0:T(8,128)(2,1)S(1)}, u32[]{:S(2)}, u32[]{:S(2)}) collective-permute-start(bf16[8,2048]{1,0:T(8,128)(2,1)S(1)} %reduce_sum.12), channel_id=1, source_target_pairs={{0,64},{64,0},{128,192},{192,128},{1,65},{65,1},{129,193},{193,129... | collective-permute-start | bytes 98312 | tf_op jit(solution)/shard_map/ppermute | solution.py:352
  133.8 10.0 %collective-permute-start.6 = (bf16[8,2048]{1,0:T(8,128)(2,1)S(1)}, bf16[8,2048]{1,0:T(8,128)(2,1)S(1)}, u32[]{:S(2)}, u32[]{:S(2)}) collective-permute-start(bf16[8,2048]{1,0:T(8,128)(2,1)S(1)} %add_convert_fusion.3), channel_id=1, source_target_pairs={{0,128},{64,192},{128,0},{192,64},{1,129},{65,193},{129,1},{193,65... | collective-permute-start | bytes 98312 | tf_op jit(solution)/shard_map/ppermute | solution.py:352
  162.2 6.0 %collective-permute-start.7 = (bf16[256,2048]{1,0:T(8,128)(2,1)S(1)}, bf16[256,2048]{1,0:T(8,128)(2,1)S(1)}, u32[]{:S(2)}, u32[]{:S(2)}) collective-permute-start(bf16[256,2048]{1,0:T(8,128)(2,1)S(1)} %bitcast.8), channel_id=1, source_target_pairs={{0,32},{32,0},{1,33},{33,1},{2,34},{34,2},{3,35},{35,3},{4,36},{36... | collective-permute-start | bytes 3145736 | tf_op jit(solution)/shard_map/ppermute | solution.py:354
